TPU v7x, 32 devices: a whole 2x2x4 slice. The times are simulated.
32 devices in a mesh: ctx: 2 (over y), exp: 16 (over z, x, core).
Axes of the slice: x: 2, y: 2, z: 4, core: 2. Of those that a mesh axis runs over, the one named last changes fastest.
Arguments:
- queries: bfloat16 [256, 64, 576], P('ctx', 'exp'), may hold values from -16 to 16
- prior_codes: bfloat16 [768, 576], P('ctx'), may hold values from -4 to 4
- fresh_codes: bfloat16 [256, 576], P('ctx'), may hold values from -4 to 4
- prior_powers: int32 [6], P('ctx'), may hold values from -1 to 1
- fresh_powers: int32 [2], P('ctx'), may hold values from -1 to 1
- block_mask: int32 [2, 8], replicated, may hold values from 0 to 1, as said below
- value_up: bfloat16 [64, 512, 128], P('exp'), may hold values from -0.25 to 0.25
- output_weight: bfloat16 [8192, 7168], P('exp'), may hold values from -0.0625 to 0.0625
- residual: bfloat16 [256, 7168], P(('ctx', 'exp')), may hold values from -2 to 2
- norm_gain: bfloat16 [7168], replicated, may hold values from 0.5 to 1.5
- router: bfloat16 [7168, 16], replicated, may hold values from -0.0625 to 0.0625
- route_ids: int32 [256, 2], P(('ctx', 'exp')), may hold values from 0 to 15, all different within a row; in each aligned block of 8 rows (0 to 7, 8 to 15, ...) at most 2 rows name the same one
- gate_weight: bfloat16 [16, 7168, 2048], P('exp', None, 'ctx'), may hold values from -0.0625 to 0.0625
- up_weight: bfloat16 [16, 7168, 2048], P('exp', None, 'ctx'), may hold values from -0.0625 to 0.0625
- down_weight: bfloat16 [16, 2048, 7168], P('exp', 'ctx'), may hold values from -0.125 to 0.125
Outputs:
- layer_out: bfloat16 [256, 7168], P(('ctx', 'exp'))
Inputs may be any that keep to these rules, and one draw needn't show every extreme that they name: block_mask[q, k] is 1 exactly when key block k (the prior blocks first, then the new ones) lies in the same document as new block q and not after it; every new block sees itself. `route_ids`: the 8 tokens of one device name one expert at most 2 times in all.
All inputs are finite; a program needn't handle non-finite values.
Results may differ from a plain program's by a relative error of at most 0.034.
Values may be sent and summed in bfloat16 or wider, within the bound.
A program may use at most 128 MiB of HBM per device.

v0:
```python
import jax
import jax.numpy as jnp
from jax import lax
from jax.sharding import PartitionSpec as P

ROPE = 64
NOPE = 128


def shifted(value, axis, by):
    devices = lax.axis_size(axis)
    return lax.ppermute(value, axis, [(i, (i + by) % devices) for i in range(devices)])


def power_two(powers):
    return jnp.where(powers < 0, 0.5, jnp.where(powers > 0, 2.0, 1.0)).astype(jnp.float32)


def expert_rows(token_rows, gate_part, up_part, down_part):
    gate_proj = jnp.dot(token_rows, gate_part, preferred_element_type=jnp.float32)
    up_proj = jnp.dot(token_rows, up_part, preferred_element_type=jnp.float32)
    inner_act = (jax.nn.silu(gate_proj) * up_proj).astype(jnp.bfloat16)
    return jnp.dot(inner_act, down_part, preferred_element_type=jnp.float32).astype(jnp.bfloat16)


def on_device(
    queries,
    prior_codes,
    fresh_codes,
    prior_powers,
    fresh_powers,
    block_mask,
    value_up,
    output_weight,
    residual,
    norm_gain,
    router,
    route_ids,
    gate_weight,
    up_weight,
    down_weight,
):
    ctx_count = lax.axis_size("ctx")
    ctx_index = lax.axis_index("ctx")
    rows_block, head_count, key_width = queries.shape
    prior_blocks = prior_powers.shape[0]
    latent_width = value_up.shape[1]
    factor = 1.0 / (NOPE + ROPE) ** 0.5
    code_rows = jnp.concatenate([prior_codes, fresh_codes], axis=0)
    scales = power_two(jnp.concatenate([prior_powers, fresh_powers], axis=0)).astype(jnp.bfloat16)
    mask_row = lax.dynamic_index_in_dim(block_mask, ctx_index, 0, keepdims=False)
    query_pos = jnp.arange(rows_block)
    causal = query_pos[:, None] >= query_pos[None, :]

    def add_block(softmax_state, key_rows, weight_scale, allowed):
        row_top, row_total, mixture = softmax_state
        scores = jnp.einsum(
            "qhd,kd->qhk", queries, key_rows, preferred_element_type=jnp.float32
        ) * (factor * weight_scale)
        scores = jnp.where(allowed[:, None, :], scores, -1e30)
        new_top = jnp.maximum(row_top, jnp.max(scores, axis=2))
        shrink = jnp.exp(row_top - new_top)
        weights = jnp.where(allowed[:, None, :], jnp.exp(scores - new_top[:, :, None]), 0.0)
        row_total = row_total * shrink + jnp.sum(weights, axis=2)
        values = jnp.einsum(
            "qhk,kl->qhl",
            weights.astype(jnp.bfloat16),
            key_rows[:, :latent_width],
            preferred_element_type=jnp.float32,
        )
        mixture = mixture * shrink[:, :, None] + values * weight_scale
        return (new_top, row_total, mixture)

    def absorb(softmax_state, owner_index, codes_now, scales_now):
        for block_number in range(prior_blocks + 1):
            if block_number < prior_blocks:
                global_block = owner_index * prior_blocks + block_number
            else:
                global_block = prior_blocks * ctx_count + owner_index
            block_live = lax.dynamic_index_in_dim(mask_row, global_block, 0, keepdims=False) > 0
            key_rows = codes_now[block_number * rows_block : (block_number + 1) * rows_block]
            weight_scale = scales_now[block_number].astype(jnp.float32)
            if block_number == prior_blocks:
                allowed = jnp.logical_and(
                    block_live, jnp.logical_or(owner_index != ctx_index, causal)
                )
            else:
                allowed = jnp.broadcast_to(block_live, (rows_block, rows_block))
            softmax_state = add_block(softmax_state, key_rows, weight_scale, allowed)
        return softmax_state

    softmax_state = (
        jnp.full((rows_block, head_count), -1e30, jnp.float32),
        jnp.zeros((rows_block, head_count), jnp.float32),
        jnp.zeros((rows_block, head_count, latent_width), jnp.float32),
    )
    softmax_state = absorb(softmax_state, ctx_index, code_rows, scales)

    def cycle_turn(turn_index, cycle_carry):
        current, codes_now, scales_now = cycle_carry
        codes_now, scales_now = shifted((codes_now, scales_now), "ctx", 1)
        owner_index = (ctx_index - turn_index) % ctx_count
        current = absorb(current, owner_index, codes_now, scales_now)
        return (current, codes_now, scales_now)

    softmax_state, code_rows, scales = lax.fori_loop(
        1, ctx_count, cycle_turn, (softmax_state, code_rows, scales)
    )
    row_top, row_total, mixture = softmax_state
    attended = (mixture / row_total[:, :, None]).astype(jnp.bfloat16)
    per_head = jnp.einsum(
        "qhl,hlv->qhv", attended, value_up, preferred_element_type=jnp.float32
    ).astype(jnp.bfloat16)
    flat_heads = per_head.reshape(rows_block, head_count * value_up.shape[2])
    head_term = jnp.dot(flat_heads, output_weight, preferred_element_type=jnp.float32)
    attention = lax.psum_scatter(
        head_term.astype(jnp.bfloat16), "exp", scatter_dimension=0, tiled=True
    ).astype(jnp.float32)
    hidden = (residual.astype(jnp.float32) + attention).astype(jnp.bfloat16)
    hidden_wide = hidden.astype(jnp.float32)
    normed = (
        hidden_wide
        * lax.rsqrt(jnp.mean(hidden_wide * hidden_wide, axis=1, keepdims=True) + 1e-06)
        * norm_gain.astype(jnp.float32)
    ).astype(jnp.bfloat16)
    expert_count = router.shape[1]
    token_count, route_count = route_ids.shape
    model_width = normed.shape[1]
    capacity = token_count * route_count * 2 // expert_count
    affinity = jax.nn.sigmoid(jnp.dot(normed, router, preferred_element_type=jnp.float32))
    route_hits = route_ids[:, :, None] == jnp.arange(expert_count)[None, None, :]
    chosen = jnp.sum(jnp.where(route_hits, affinity[:, None, :], 0.0), axis=2)
    gate_values = 2.5 * chosen / jnp.sum(chosen, axis=1, keepdims=True)
    flat_hits = route_hits.reshape(token_count * route_count, expert_count).astype(jnp.int32)
    before = jnp.cumsum(flat_hits, axis=0) - flat_hits
    slot_index = jnp.sum(before * flat_hits, axis=1)
    target = route_ids.reshape(-1) * capacity + slot_index
    placing = (target[None, :] == jnp.arange(expert_count * capacity)[:, None]).astype(jnp.bfloat16)
    repeated = jnp.repeat(normed, route_count, axis=0)
    buffer = jnp.dot(placing, repeated, preferred_element_type=jnp.float32).astype(jnp.bfloat16)
    gate_part = gate_weight[0]
    up_part = up_weight[0]
    down_part = down_weight[0]
    sectioned = lax.all_to_all(
        buffer.reshape(expert_count, capacity, model_width),
        "exp",
        split_axis=0,
        concat_axis=0,
        tiled=True,
    )
    partials = expert_rows(
        lax.all_gather(
            sectioned.reshape(expert_count * capacity, model_width), "ctx", axis=0, tiled=True
        ),
        gate_part,
        up_part,
        down_part,
    )
    partials = partials.reshape(ctx_count * expert_count, capacity, model_width)
    returned = lax.all_to_all(partials, ("ctx", "exp"), split_axis=0, concat_axis=0, tiled=True)
    summed = jnp.sum(
        returned.reshape(ctx_count, expert_count * capacity, model_width).astype(jnp.float32),
        axis=0,
    ).astype(jnp.bfloat16)
    gathered_back = jnp.dot(
        jnp.transpose(placing), summed, preferred_element_type=jnp.float32
    ).reshape(token_count, route_count, model_width)
    expert_mix = jnp.sum(gate_values[:, :, None] * gathered_back, axis=1)
    return (hidden_wide + expert_mix).astype(jnp.bfloat16)


def solution(mesh):
    in_specs = (
        P("ctx", "exp", None),
        P("ctx", None),
        P("ctx", None),
        P("ctx"),
        P("ctx"),
        P(),
        P("exp", None, None),
        P("exp", None),
        P(("ctx", "exp"), None),
        P(),
        P(),
        P(("ctx", "exp"), None),
        P("exp", None, "ctx"),
        P("exp", None, "ctx"),
        P("exp", "ctx", None),
    )
    out_specs = P(("ctx", "exp"), None)
    return jax.shard_map(
        on_device, mesh=mesh, in_specs=in_specs, out_specs=out_specs, check_vma=False
    )
```

profile of v0, /device:TPU:0, one launch (start us, length us, event | category | flops | bytes accessed | tf_op | source)
XLA Modules:
  0.0 210.0 jit_solution(10697159546850577400)
XLA Ops:
  6.5 1.2 pad_maximum_fusion
  7.8 3.0 %collective-permute-start = (bf16[512,576]{0,1:T(8,128)(2,1)S(1)}, bf16[512,576]{0,1:T(8,128)(2,1)S(1)}, u32[]{:S(2)}, u32[]{:S(2)}) collective-permute-start(bf16[512,576]{0,1:T(8,128)(2,1)S(1)} %pad_maximum_fusion), channel_id=1, source_target_pairs={{0,16},{16,0},{1,17},{17,1},{2,18},{18,2},{3,19},{19,3},{4,20},{20... | collective-permute-start | bytes 1769480 | tf_op jit(solution)/shard_map/while/body/eval_jaxpr/ppermute | solution.py:12
  11.4 0.7 fusion.141
  12.2 0.7 fusion.156
  18.0 1.7 fusion.155
  24.7 1.2 fusion.163
  25.9 1.2 fusion.164
  27.2 1.2 fusion.165
  28.4 1.2 fusion.162
  29.7 0.7 fusion.157
  36.7 1.3 convolution_multiply_fusion.7
  38.1 1.2 convolution_multiply_fusion.6
  39.7 1.4 fusion.14
  41.1 1.3 fusion.16
  42.5 0.3 convolution_multiply_fusion.3
  42.8 1.4 convolution_multiply_fusion.2
  44.2 1.3 convolution_multiply_fusion.1
  45.5 2.7 %fusion.46 = bf16[4,128,128]{1,2,0:T(8,128)(2,1)S(1)} fusion(bf16[4,512,128]{2,1,0:T(8,128)(2,1)S(1)} %copy-done.8, f32[128,4,512]{2,0,1:T(8,128)} %convolution_multiply_fusion.1, f32[128,4,512]{2,0,1:T(8,128)} %convolution_multiply_fusion.2, f32[128,4,512]{2,0,1:T(8,128)S(1)} %convolution_multiply_fusion.3, f32[128,4,512]{2,0,1:T(8,128)} %fusion.16, ...), kind=kOutput, calls=%fused_computation.59 | convolution fusion | flops 137101312 | bytes 5253125 | tf_op jit(solution)/shard_map/qhl,hlv->qhv/dot_general | solution.py:111
  48.2 5.5 %convolution_convert_fusion = bf16[128,7168]{1,0:T(8,128)(2,1)} fusion(bf16[128,512]{0,1:T(8,128)(2,1)S(1)} %bitcast.142, bf16[512,7168]{1,0:T(8,128)(2,1)} %param.22), kind=kOutput, calls=%fused_computation.6 | convolution fusion | flops 940441600 | bytes 9306112 | tf_op jit(solution)/shard_map/dot_general | solution.py:115
  54.2 61.9 %reduce-scatter.2.cloned.1.call-done = bf16[8,7168]{1,0:T(8,128)(2,1)} async-done(((bf16[128,7168]{1,0:T(8,128)(2,1)}), bf16[8,7168]{1,0:T(8,128)(2,1)}) %reduce-scatter.2.cloned.1.call-update) | async-done | bytes 114704 | tf_op jit(solution)/shard_map/reduce_scatter | solution.py:116
  116.2 1.1 fusion.63
  117.2 1.0 fusion.65
  118.9 16.7 %all_to_all.10 = bf16[16,2,7168]{2,1,0:T(2,128)(2,1)S(1)} all-to-all(bf16[16,2,7168]{2,1,0:T(2,128)(2,1)S(1)} %reshape.358), channel_id=1, replica_groups=mesh['ctx'=2,'exp'=16] {'exp'}, dimensions={0} | all-to-all | bytes 917504 | tf_op jit(solution)/shard_map/all_to_all | solution.py:144
  135.8 13.4 %all_gather.3 = bf16[64,7168]{1,0:T(8,128)(2,1)S(1)} all-gather(bf16[32,7168]{1,0:T(8,128)(2,1)S(1)} %reshape.359), channel_id=1, replica_groups=mesh['ctx'=2,'exp'=16] {'ctx'}, dimensions={0}, use_global_device_ids=true | all-gather | bytes 1376256 | tf_op jit(solution)/shard_map/all_gather | solution.py:152
  149.2 7.9 %fusion.4 = f32[64,1024]{1,0:T(8,128)S(1)} fusion(bf16[64,7168]{1,0:T(8,128)(2,1)S(1)} %all_gather.3, bf16[1,7168,1024]{2,1,0:T(8,128)(2,1)} %param.27), kind=kOutput, calls=%fused_computation.4 | convolution fusion | flops 939524096 | bytes 15859712 | tf_op jit(solution)/shard_map/dot_general | solution.py:20
  157.1 14.6 %fusion.6 = bf16[64,7168]{1,0:T(8,128)(2,1)S(1)} fusion(bf16[1,1024,7168]{2,1,0:T(8,128)(2,1)} %param.29, bf16[64,7168]{1,0:T(8,128)(2,1)S(1)} %all_gather.3, bf16[1,7168,1024]{2,1,0:T(8,128)(2,1)} %param.28, f32[64,1024]{1,0:T(8,128)S(1)} %fusion.4), kind=kOutput, calls=%fused_computation.7 | convolution fusion | flops 1879900160 | bytes 31457280 | tf_op jit(solution)/shard_map/dot_general | solution.py:23
  171.8 1.3 reshape.360
  173.0 4.0 %all-to-all-start.1 = ((bf16[32,2,7168]{2,1,0:T(2,128)(2,1)}), bf16[32,2,7168]{2,1,0:T(2,128)(2,1)S(1)}, u32[]{:S(2)}, u32[]{:S(2)}) async-start(bf16[32,2,7168]{2,1,0:T(2,128)(2,1)} %reshape.360), calls=%async_computation.2 | async-start | bytes 1835008 | tf_op jit(solution)/shard_map/all_to_all | solution.py:160
  177.6 23.8 %all-to-all-done.1 = bf16[32,2,7168]{2,1,0:T(2,128)(2,1)S(1)} async-done(((bf16[32,2,7168]{2,1,0:T(2,128)(2,1)}), bf16[32,2,7168]{2,1,0:T(2,128)(2,1)S(1)}, u32[]{:S(2)}, u32[]{:S(2)}) %all-to-all-start.1) | async-done | bytes 917536 | tf_op jit(solution)/shard_map/all_to_all | solution.py:160
  201.4 0.3 reshape.361
  201.8 0.4 reduce_sum.148
  202.4 0.7 fusion.66
  (55 shorter events, 4.0 us)
Async XLA Ops:
  6.5 18.2 %copy-start = (bf16[128,4,576]{0,2,1:T(8,128)(2,1)S(1)}, bf16[128,4,576]{0,2,1:T(8,128)(2,1)}, u32[]{:S(2)}) copy-start(bf16[128,4,576]{0,2,1:T(8,128)(2,1)} %param.15) | copy-start | bytes 1769476
  6.5 34.6 %copy-start.4 = (bf16[128,576]{0,1:T(8,128)(2,1)S(1)}, bf16[128,576]{0,1:T(8,128)(2,1)}, u32[]{:S(2)}) copy-start(bf16[128,576]{0,1:T(8,128)(2,1)} %param.17) | copy-start | bytes 442372
  6.5 109.6 %reduce-scatter.2.cloned.1.call-start = ((), (), s32[]{:S(2)}) async-start(), calls=%async_computation.3 | async-start | bytes 1949696 | tf_op jit(solution)/shard_map/reduce_scatter | solution.py:116
  7.8 27.6 %collective-permute-start = (bf16[512,576]{0,1:T(8,128)(2,1)S(1)}, bf16[512,576]{0,1:T(8,128)(2,1)S(1)}, u32[]{:S(2)}, u32[]{:S(2)}) collective-permute-start(bf16[512,576]{0,1:T(8,128)(2,1)S(1)} %pad_maximum_fusion), channel_id=1, source_target_pairs={{0,16},{16,0},{1,17},{17,1},{2,18},{18,2},{3,19},{19,3},{4,20},{20... | collective-permute-start | bytes 1769480 | tf_op jit(solution)/shard_map/while/body/eval_jaxpr/ppermute | solution.py:12
  12.2 17.5 %collective-permute-start.1 = (bf16[4]{0:T(256)(128)(2,1)S(1)}, bf16[4]{0:T(256)(128)(2,1)S(1)}, u32[]{:S(2)}, u32[]{:S(2)}) collective-permute-start(bf16[4]{0:T(256)(128)(2,1)S(1)} %fusion.141), channel_id=1, source_target_pairs={{0,16},{16,0},{1,17},{17,1},{2,18},{18,2},{3,19},{19,3},{4,20},{20... | collective-permute-start | bytes 32 | tf_op jit(solution)/shard_map/while/body/eval_jaxpr/ppermute | solution.py:12
  36.6 8.9 %copy-start.8 = (bf16[4,512,128]{2,1,0:T(8,128)(2,1)S(1)}, bf16[4,512,128]{2,1,0:T(8,128)(2,1)}, u32[]{:S(2)}) copy-start(bf16[4,512,128]{2,1,0:T(8,128)(2,1)} %param.21) | copy-start | bytes 1572868
  41.1 12.6 %copy-start.6 = (bf16[7168]{0:T(1024)(128)(2,1)S(1)}, bf16[7168]{0:T(1024)(128)(2,1)}, u32[]{:S(2)}) copy-start(bf16[7168]{0:T(1024)(128)(2,1)} %param.24) | copy-start | bytes 43012
  41.1 12.7 %copy-start.7 = (s32[8,2]{0,1:T(2,128)S(1)}, s32[8,2]{0,1:T(2,128)}, u32[]{:S(2)}) copy-start(s32[8,2]{0,1:T(2,128)} %param.26) | copy-start | bytes 196
  41.1 75.0 %copy-start.2 = (bf16[8,7168]{1,0:T(8,128)(2,1)S(1)}, bf16[8,7168]{1,0:T(8,128)(2,1)}, u32[]{:S(2)}) copy-start(bf16[8,7168]{1,0:T(8,128)(2,1)} %param.23) | copy-start | bytes 344068
  149.2 53.9 %copy-start.1 = (bf16[128,4,576]{0,2,1:T(8,128)(2,1)S(1)}, bf16[128,4,576]{0,2,1:T(8,128)(2,1)}, u32[]{:S(2)}) copy-start(bf16[128,4,576]{0,2,1:T(8,128)(2,1)} %param.15) | copy-start | bytes 1769476
  157.1 20.1 %copy-start.5 = (bf16[7168,16]{0,1:T(8,128)(2,1)S(1)}, bf16[7168,16]{0,1:T(8,128)(2,1)}, u32[]{:S(2)}) copy-start(bf16[7168,16]{0,1:T(8,128)(2,1)} %param.25) | copy-start | bytes 688132
  157.1 45.3 %copy-start.3 = (bf16[8,7168]{1,0:T(8,128)(2,1)S(1)}, bf16[8,7168]{1,0:T(8,128)(2,1)}, u32[]{:S(2)}) copy-start(bf16[8,7168]{1,0:T(8,128)(2,1)} %reduce-scatter.2.cloned.1.call-done) | copy-start | bytes 344068
  173.0 28.4 %all-to-all-start.1 = ((bf16[32,2,7168]{2,1,0:T(2,128)(2,1)}), bf16[32,2,7168]{2,1,0:T(2,128)(2,1)S(1)}, u32[]{:S(2)}, u32[]{:S(2)}) async-start(bf16[32,2,7168]{2,1,0:T(2,128)(2,1)} %reshape.360), calls=%async_computation.2 | async-start | bytes 1835008 | tf_op jit(solution)/shard_map/all_to_all | solution.py:160
Sparse Core Ops, SparseCore 0:
  53.9 62.2 reduce-scatter.1
where the time goes:
time: 211 us; the launch traced here: 210 us
  waiting for transfers between devices  85.7 us (41%)
  matrix products  45.8 us (22%)
  blocking collectives  30.1 us (14%)
  between operations  29.5 us (14%)
  starting transfers between devices  7.01 us (3%)
  other arithmetic  6.18 us (3%)
  local copies, waits for them, and re-layouts  5.53 us (3%)
    reduce_scatter x1, waiting for transfers between devices, on_device(): lax.psum_scatter(head_term.astype(jnp.bfloat16), 'exp', scatter_dimension...  61.9 us
    all_to_all x1, waiting for transfers between devices, on_device(): lax.all_to_all(partials, ('ctx', 'exp'), split_axis=0, concat_axis=0, til...  23.8 us
    all_to_all x1, blocking collectives, on_device(): lax.all_to_all(buffer.reshape(expert_count, capacity, model_width), 'exp'...  16.7 us
    dot_general x1, matrix products, expert_rows(): jnp.dot(inner_act, down_part, preferred_element_type=jnp.float32)  14.6 us
    all_gather x1, blocking collectives, on_device(): lax.all_gather(sectioned.reshape(expert_count * capacity, model_width), '...  13.4 us
    dot_general x7, matrix products, add_block(): jnp.einsum('qhk,kl->qhl', weights.astype(jnp.bfloat16), key_rows[:, :late...  8.28 us
    dot_general x1, matrix products, expert_rows(): jnp.dot(token_rows, gate_part, preferred_element_type=jnp.float32)  7.88 us
    dot_general x8, matrix products, add_block(): jnp.einsum('qhd,kd->qhk', queries, key_rows, preferred_element_type=jnp.f...  6.17 us
  transfers between devices with their start and end apart: 4, of which 2 were waited for; matrix products, arithmetic and copies ran while one was open for 5% of the time, Pallas kernels for 0%

commit v1 on v0

v1 whole, which is shorter than its diff:
```python
import functools

import jax
import jax.numpy as jnp
from jax import lax
from jax.experimental import pallas as pl
from jax.experimental.pallas import tpu as pltpu
from jax.sharding import PartitionSpec as P

ROPE = 64
NOPE = 128
MESH = pl.DeviceIdType.MESH
CHUNKS = 4
PIECES = 8


def power_two(powers):
    return jnp.where(powers < 0, 0.5, jnp.where(powers > 0, 2.0, 1.0)).astype(jnp.float32)


def greet(peers):
    barrier = pltpu.get_barrier_semaphore()
    for peer in peers:
        pl.semaphore_signal(barrier, inc=1, device_id=peer, device_id_type=MESH)
    pl.semaphore_wait(barrier, len(peers))


def attention_kernel(
    ctx_count,
    exp_count,
    q_ref,
    lat_ref,
    mask_ref,
    up_ref,
    w_hbm,
    out_ref,
    keys,
    flat,
    w_buf,
    *rest,
):
    stages = exp_count.bit_length() - 1
    held = rest[:stages]
    landed = rest[stages : 2 * stages]
    w_sem, lat_send, lat_recv, fwd_send, fwd_recv, rs_send, rs_recv = rest[2 * stages :]
    ctx = lax.axis_index("ctx")
    exp = lax.axis_index("exp")
    heads, latent_width, vhead = up_ref.shape
    rows = q_ref.shape[0] // heads
    key_width, key_rows = lat_ref.shape
    half = key_width // 2
    model = out_ref.shape[1]
    side = model // 2
    width = side // CHUNKS
    bits = [lax.rem(exp // (1 << i), 2) for i in range(stages)]
    partners = [exp + (1 - 2 * bits[i]) * (1 << i) for i in range(stages)]

    weights_in = []
    for chunk in range(CHUNKS):
        pair = []
        for h in range(2):
            columns = pl.ds(h * side + chunk * width, width)
            copy = pltpu.make_async_copy(
                w_hbm.at[:, columns], w_buf.at[:, columns], w_sem.at[chunk, h]
            )
            copy.start()
            pair.append(copy)
        weights_in.append(pair)

    others = [lax.rem(ctx + d, ctx_count) for d in range(1, ctx_count)]
    senders = [lax.rem(ctx + ctx_count - d, ctx_count) for d in range(1, ctx_count)]
    greet([(o, exp) for o in others] + [(ctx, p) for p in partners])

    part = pl.ds(pl.multiple_of(bits[0] * half, half), half)
    sends = []
    for d, other in enumerate(others):
        copy = pltpu.make_async_remote_copy(
            src_ref=lat_ref.at[part],
            dst_ref=keys.at[ctx, part],
            send_sem=lat_send.at[d],
            recv_sem=lat_recv.at[d],
            device_id=(other, exp),
            device_id_type=MESH,
        )
        copy.start()
        sends.append(copy)
    keys[ctx] = lat_ref[...]
    forwards = []
    for d, sender in enumerate(senders):
        sends[d].wait_recv()
        copy = pltpu.make_async_remote_copy(
            src_ref=keys.at[sender, part],
            dst_ref=keys.at[sender, part],
            send_sem=fwd_send.at[d],
            recv_sem=fwd_recv.at[d],
            device_id=(ctx, partners[0]),
            device_id_type=MESH,
        )
        copy.start()
        forwards.append(copy)
    for copy in forwards:
        copy.wait_recv()

    factor = 1.0 / (NOPE + ROPE) ** 0.5
    for h in range(heads):
        q_head = q_ref[h * rows : (h + 1) * rows, :]
        scores = []
        for o in range(ctx_count):
            raw = jnp.dot(q_head, keys[o], preferred_element_type=jnp.float32) * factor
            live = mask_ref[:, o * key_rows : (o + 1) * key_rows] > 0
            scores.append(jnp.where(live, raw, -1e30))
        top = jnp.max(scores[0], axis=1, keepdims=True)
        for s in scores[1:]:
            top = jnp.maximum(top, jnp.max(s, axis=1, keepdims=True))
        total = jnp.zeros((rows, 1), jnp.float32)
        mixture = jnp.zeros((rows, latent_width), jnp.float32)
        for o in range(ctx_count):
            live = mask_ref[:, o * key_rows : (o + 1) * key_rows] > 0
            weights = jnp.where(live, jnp.exp(scores[o] - top), 0.0)
            total = total + jnp.sum(weights, axis=1, keepdims=True)
            mixture = mixture + lax.dot_general(
                weights.astype(jnp.bfloat16),
                keys[o, :latent_width, :],
                (((1,), (1,)), ((), ())),
                preferred_element_type=jnp.float32,
            )
        attended = (mixture / total).astype(jnp.bfloat16)
        head_out = jnp.dot(attended, up_ref[h], preferred_element_type=jnp.float32)
        flat[:, h * vhead : (h + 1) * vhead] = head_out.astype(jnp.bfloat16)

    tokens = rows // exp_count

    def exchange(stage, chunk):
        return pltpu.make_async_remote_copy(
            src_ref=held[stage].at[chunk, :, 1 - bits[stage]],
            dst_ref=landed[stage].at[chunk],
            send_sem=rs_send.at[stage, chunk],
            recv_sem=rs_recv.at[stage, chunk],
            device_id=(ctx, partners[stage]),
            device_id_type=MESH,
        )

    for turn in range(CHUNKS + stages):
        if turn < CHUNKS:
            sides = []
            for h in range(2):
                weights_in[turn][h].wait()
                at = h * side + turn * width
                term = jnp.dot(
                    flat[...], w_buf[:, at : at + width], preferred_element_type=jnp.float32
                )
                sides.append(term.reshape(exp_count, tokens, width))
            both = jnp.concatenate(sides, axis=1).astype(jnp.bfloat16)
            held[0][turn] = both.reshape(exp_count // 2, 2, 2 * tokens, width)
            exchange(0, turn).start()
        for stage in reversed(range(stages)):
            chunk = turn - 1 - stage
            if chunk < 0 or chunk >= CHUNKS:
                continue
            exchange(stage, chunk).wait_recv()
            mine = held[stage][chunk, :, pl.ds(bits[stage], 1)]
            count = mine.shape[0]
            summed = mine.reshape(count, 2 * tokens, width).astype(jnp.float32)
            summed = summed + landed[stage][chunk].astype(jnp.float32)
            if stage + 1 < stages:
                held[stage + 1][chunk] = summed.astype(jnp.bfloat16).reshape(
                    count // 2, 2, 2 * tokens, width
                )
                exchange(stage + 1, chunk).start()
            else:
                last = summed.reshape(2 * tokens, width)
                for h in range(2):
                    at = h * side + chunk * width
                    out_ref[:, at : at + width] = last[h * tokens : (h + 1) * tokens, :]
    for d in range(ctx_count - 1):
        sends[d].wait_send()
        forwards[d].wait_send()
    for stage in range(stages):
        for chunk in range(CHUNKS):
            exchange(stage, chunk).wait_send()


def attention_call(ctx_count, exp_count, q_rows, latent_t, mask, value_up, output_weight):
    heads, latent_width, vhead = value_up.shape
    rows = q_rows.shape[0] // heads
    key_width, key_rows = latent_t.shape
    model = output_weight.shape[1]
    tokens = rows // exp_count
    stages = exp_count.bit_length() - 1
    width = model // 2 // CHUNKS
    vmem = pl.BlockSpec(memory_space=pltpu.VMEM)
    scratch = [
        pltpu.VMEM((ctx_count, key_width, key_rows), jnp.bfloat16),
        pltpu.VMEM((rows, heads * vhead), jnp.bfloat16),
        pltpu.VMEM(output_weight.shape, jnp.bfloat16),
    ]
    for stage in range(stages):
        blocks = exp_count >> (stage + 1)
        scratch.append(pltpu.VMEM((CHUNKS, blocks, 2, 2 * tokens, width), jnp.bfloat16))
    for stage in range(stages):
        blocks = exp_count >> (stage + 1)
        scratch.append(pltpu.VMEM((CHUNKS, blocks, 2 * tokens, width), jnp.bfloat16))
    dma = pltpu.SemaphoreType.DMA
    scratch += [
        dma((CHUNKS, 2)),
        dma((ctx_count - 1,)),
        dma((ctx_count - 1,)),
        dma((ctx_count - 1,)),
        dma((ctx_count - 1,)),
        dma((stages, CHUNKS)),
        dma((stages, CHUNKS)),
    ]
    return pl.pallas_call(
        functools.partial(attention_kernel, ctx_count, exp_count),
        out_shape=jax.ShapeDtypeStruct((tokens, model), jnp.float32),
        in_specs=[vmem, vmem, vmem, vmem, pl.BlockSpec(memory_space=pl.ANY)],
        out_specs=vmem,
        scratch_shapes=scratch,
        compiler_params=pltpu.CompilerParams(
            collective_id=0, has_side_effects=True, vmem_limit_bytes=48 << 20
        ),
    )(q_rows, latent_t, mask, value_up, output_weight)


def expert_kernel(
    ctx_count,
    exp_count,
    buf_ref,
    gate_hbm,
    up_hbm,
    down_hbm,
    out_ref,
    gate_w,
    up_w,
    down_w,
    recv,
    rows_in,
    ret_in,
    out_buf,
    w_sem,
    d_send,
    d_recv,
    f_send,
    f_recv,
    r_send,
    r_recv,
    b_send,
    b_recv,
):
    ctx = lax.axis_index("ctx")
    exp = lax.axis_index("exp")
    width = buf_ref.shape[2]
    block = buf_ref.shape[1]
    slots = exp_count * block // PIECES
    weights_in = []
    for which, (source, target) in enumerate(((gate_hbm, gate_w), (up_hbm, up_w))):
        for piece in range(PIECES):
            span = pl.ds(piece * width, width)
            weights_in.append(
                pltpu.make_async_copy(
                    source.at[0, span], target.at[span], w_sem.at[which, piece]
                )
            )
    for piece in range(PIECES):
        span = pl.ds(piece * width, width)
        weights_in.append(
            pltpu.make_async_copy(
                down_hbm.at[0, :, span], down_w.at[:, span], w_sem.at[2, piece]
            )
        )
    for copy in weights_in:
        copy.start()

    order = sorted(range(1, exp_count), key=lambda k: abs(k - exp_count // 2))
    to = {k: lax.rem(exp + k, exp_count) for k in range(exp_count)}
    origin = {k: lax.rem(exp + exp_count - k, exp_count) for k in range(exp_count)}
    others = [lax.rem(ctx + d, ctx_count) for d in range(1, ctx_count)]
    senders = [lax.rem(ctx + ctx_count - d, ctx_count) for d in range(1, ctx_count)]
    greet([(ctx, to[k]) for k in order] + [(o, exp) for o in others])

    def dispatch(k):
        return pltpu.make_async_remote_copy(
            src_ref=buf_ref.at[to[k]],
            dst_ref=recv.at[ctx, exp],
            send_sem=d_send.at[k],
            recv_sem=d_recv.at[k],
            device_id=(ctx, to[k]),
            device_id_type=MESH,
        )

    def forward(d, k):
        return pltpu.make_async_remote_copy(
            src_ref=recv.at[ctx, origin[k]],
            dst_ref=recv.at[ctx, origin[k]],
            send_sem=f_send.at[d, k],
            recv_sem=f_recv.at[d, k],
            device_id=(others[d], exp),
            device_id_type=MESH,
        )

    def give_back(d, k):
        return pltpu.make_async_remote_copy(
            src_ref=recv.at[others[d], to[k]],
            dst_ref=ret_in.at[d, to[k]],
            send_sem=r_send.at[d, k],
            recv_sem=r_recv.at[d, k],
            device_id=(others[d], exp),
            device_id_type=MESH,
        )

    def hand_in(k):
        return pltpu.make_async_remote_copy(
            src_ref=out_buf.at[to[k]],
            dst_ref=out_ref.at[exp],
            send_sem=b_send.at[k],
            recv_sem=b_recv.at[k],
            device_id=(ctx, to[k]),
            device_id_type=MESH,
        )

    for k in order:
        dispatch(k).start()
    recv[ctx, exp] = buf_ref[exp]
    for d in range(ctx_count - 1):
        forward(d, 0).start()
    arrival = sorted(range(1, exp_count), key=lambda k: min(k, exp_count - k))
    for k in arrival:
        dispatch(k).wait_recv()
        for d in range(ctx_count - 1):
            forward(d, k).start()

    row = lax.broadcasted_iota(jnp.int32, (exp_count * block, exp_count * block), 0)
    column = lax.broadcasted_iota(jnp.int32, (exp_count * block, exp_count * block), 1)
    split = jnp.where(
        column == lax.rem(row, slots) * PIECES + row // slots, 1.0, 0.0
    ).astype(jnp.bfloat16)
    merge = jnp.where(
        row == lax.rem(column, slots) * PIECES + column // slots, 1.0, 0.0
    ).astype(jnp.bfloat16)

    def spread(which):
        packed = recv[which].reshape(exp_count * block, width)
        apart = jnp.dot(split, packed, preferred_element_type=jnp.float32).astype(jnp.bfloat16)
        at = pl.ds(pl.multiple_of(which * slots, slots), slots)
        for piece in range(PIECES):
            rows_in[piece, at, :] = apart[piece * slots : (piece + 1) * slots, :]

    spread(ctx)
    for d in range(ctx_count - 1):
        for k in [0] + arrival:
            forward(d, k).wait_recv()
        spread(senders[d])

    gate = None
    up = None
    for piece in range(PIECES):
        weights_in[piece].wait()
        weights_in[PIECES + piece].wait()
        span = slice(piece * width, (piece + 1) * width)
        rows = rows_in[piece]
        gate_part = jnp.dot(rows, gate_w[span, :], preferred_element_type=jnp.float32)
        up_part = jnp.dot(rows, up_w[span, :], preferred_element_type=jnp.float32)
        gate = gate_part if gate is None else gate + gate_part
        up = up_part if up is None else up + up_part
    inner = (gate / (1.0 + jnp.exp(-gate)) * up).astype(jnp.bfloat16)
    for piece in range(PIECES):
        weights_in[2 * PIECES + piece].wait()
        span = slice(piece * width, (piece + 1) * width)
        result = jnp.dot(inner, down_w[:, span], preferred_element_type=jnp.float32)
        rows_in[piece] = result.astype(jnp.bfloat16)

    for k in order:
        dispatch(k).wait_send()
    for d in range(ctx_count - 1):
        for k in range(exp_count):
            forward(d, k).wait_send()

    def gather(which):
        at = pl.ds(pl.multiple_of(which * slots, slots), slots)
        apart = jnp.concatenate([rows_in[piece, at, :] for piece in range(PIECES)], axis=0)
        packed = jnp.dot(merge, apart, preferred_element_type=jnp.float32).astype(jnp.bfloat16)
        recv[which] = packed.reshape(exp_count, block, width)

    for d in range(ctx_count - 1):
        gather(others[d])
        for k in order + [0]:
            give_back(d, k).start()
    gather(ctx)
    for k in order + [0]:
        total = recv[ctx, to[k]].astype(jnp.float32)
        for d in range(ctx_count - 1):
            give_back(d, k).wait_recv()
            total = total + ret_in[d, to[k]].astype(jnp.float32)
        if k == 0:
            out_ref[exp] = total.astype(jnp.bfloat16)
        else:
            out_buf[to[k]] = total.astype(jnp.bfloat16)
            hand_in(k).start()
    for k in order:
        hand_in(k).wait_recv()
    for k in order:
        hand_in(k).wait_send()
    for d in range(ctx_count - 1):
        for k in range(exp_count):
            give_back(d, k).wait_send()


def expert_call(ctx_count, exp_count, buffer, gate_weight, up_weight, down_weight):
    block, width = buffer.shape[1:]
    model, hidden = gate_weight.shape[1:]
    slots = exp_count * block // PIECES
    vmem = pl.BlockSpec(memory_space=pltpu.VMEM)
    anywhere = pl.BlockSpec(memory_space=pl.ANY)
    dma = pltpu.SemaphoreType.DMA
    return pl.pallas_call(
        functools.partial(expert_kernel, ctx_count, exp_count),
        out_shape=jax.ShapeDtypeStruct(buffer.shape, jnp.bfloat16),
        in_specs=[vmem, anywhere, anywhere, anywhere],
        out_specs=vmem,
        scratch_shapes=[
            pltpu.VMEM((model, hidden), jnp.bfloat16),
            pltpu.VMEM((model, hidden), jnp.bfloat16),
            pltpu.VMEM((hidden, model), jnp.bfloat16),
            pltpu.VMEM((ctx_count, exp_count, block, width), jnp.bfloat16),
            pltpu.VMEM((PIECES, ctx_count * slots, width), jnp.bfloat16),
            pltpu.VMEM((ctx_count - 1, exp_count, block, width), jnp.bfloat16),
            pltpu.VMEM((exp_count, block, width), jnp.bfloat16),
            dma((3, PIECES)),
            dma((exp_count,)),
            dma((exp_count,)),
            dma((ctx_count - 1, exp_count)),
            dma((ctx_count - 1, exp_count)),
            dma((ctx_count - 1, exp_count)),
            dma((ctx_count - 1, exp_count)),
            dma((exp_count,)),
            dma((exp_count,)),
        ],
        compiler_params=pltpu.CompilerParams(
            collective_id=1, has_side_effects=True, vmem_limit_bytes=62 << 20
        ),
    )(buffer, gate_weight, up_weight, down_weight)


def on_device(
    queries,
    prior_codes,
    fresh_codes,
    prior_powers,
    fresh_powers,
    block_mask,
    value_up,
    output_weight,
    residual,
    norm_gain,
    router,
    route_ids,
    gate_weight,
    up_weight,
    down_weight,
):
    ctx_count = lax.axis_size("ctx")
    exp_count = lax.axis_size("exp")
    ctx_index = lax.axis_index("ctx")
    rows_block, head_count, key_width = queries.shape
    prior_blocks = prior_powers.shape[0]
    own_blocks = prior_blocks + 1
    scales = power_two(jnp.concatenate([prior_powers, fresh_powers], axis=0))
    code_rows = jnp.concatenate([prior_codes, fresh_codes], axis=0)
    latent_t = (
        code_rows.T.astype(jnp.float32) * jnp.repeat(scales, rows_block)[None, :]
    ).astype(jnp.bfloat16)
    q_rows = queries.transpose(1, 0, 2).reshape(head_count * rows_block, key_width)

    mask_row = lax.dynamic_index_in_dim(block_mask, ctx_index, 0, keepdims=False)
    prior_mask = mask_row[: prior_blocks * ctx_count].reshape(ctx_count, prior_blocks)
    fresh_mask = mask_row[prior_blocks * ctx_count :].reshape(ctx_count, 1)
    live = jnp.concatenate([prior_mask, fresh_mask], axis=1) > 0
    position = jnp.arange(rows_block)
    is_fresh = jnp.arange(own_blocks)[None, :] == prior_blocks
    is_own = jnp.arange(ctx_count)[:, None] == ctx_index
    diagonal = jnp.logical_and(is_fresh, is_own)
    causal = position[:, None] >= position[None, :]
    later = jnp.logical_and(is_fresh, jnp.arange(ctx_count)[:, None] > ctx_index)
    live = jnp.logical_and(live, jnp.logical_not(later))
    allowed = jnp.logical_and(
        live[None, :, :, None],
        jnp.logical_or(jnp.logical_not(diagonal)[None, :, :, None], causal[:, None, None, :]),
    )
    mask = allowed.reshape(rows_block, ctx_count * own_blocks * rows_block).astype(jnp.float32)

    attention = attention_call(
        ctx_count, exp_count, q_rows, latent_t, mask, value_up, output_weight
    )
    hidden = (residual.astype(jnp.float32) + attention).astype(jnp.bfloat16)
    hidden_wide = hidden.astype(jnp.float32)
    normed = (
        hidden_wide
        * lax.rsqrt(jnp.mean(hidden_wide * hidden_wide, axis=1, keepdims=True) + 1e-06)
        * norm_gain.astype(jnp.float32)
    ).astype(jnp.bfloat16)
    expert_count = router.shape[1]
    token_count, route_count = route_ids.shape
    model_width = normed.shape[1]
    capacity = token_count * route_count * 2 // expert_count
    affinity = jax.nn.sigmoid(jnp.dot(normed, router, preferred_element_type=jnp.float32))
    route_hits = route_ids[:, :, None] == jnp.arange(expert_count)[None, None, :]
    chosen = jnp.sum(jnp.where(route_hits, affinity[:, None, :], 0.0), axis=2)
    gate_values = 2.5 * chosen / jnp.sum(chosen, axis=1, keepdims=True)
    flat_hits = route_hits.reshape(token_count * route_count, expert_count).astype(jnp.int32)
    before = jnp.cumsum(flat_hits, axis=0) - flat_hits
    slot_index = jnp.sum(before * flat_hits, axis=1)
    target = route_ids.reshape(-1) * capacity + slot_index
    placing = (target[None, :] == jnp.arange(expert_count * capacity)[:, None]).astype(jnp.bfloat16)
    to_token = jnp.sum(placing.reshape(-1, token_count, route_count), axis=2)
    buffer = jnp.dot(to_token, normed, preferred_element_type=jnp.float32).astype(jnp.bfloat16)
    summed = expert_call(
        ctx_count,
        exp_count,
        buffer.reshape(expert_count, capacity * PIECES, model_width // PIECES),
        gate_weight,
        up_weight,
        down_weight,
    ).reshape(expert_count * capacity, model_width)
    gathered_back = jnp.dot(
        jnp.transpose(placing), summed, preferred_element_type=jnp.float32
    ).reshape(token_count, route_count, model_width)
    expert_mix = jnp.sum(gate_values[:, :, None] * gathered_back, axis=1)
    return (hidden_wide + expert_mix).astype(jnp.bfloat16)


def solution(mesh):
    in_specs = (
        P("ctx", "exp", None),
        P("ctx", None),
        P("ctx", None),
        P("ctx"),
        P("ctx"),
        P(),
        P("exp", None, None),
        P("exp", None),
        P(("ctx", "exp"), None),
        P(),
        P(),
        P(("ctx", "exp"), None),
        P("exp", None, "ctx"),
        P("exp", None, "ctx"),
        P("exp", "ctx", None),
    )
    out_specs = P(("ctx", "exp"), None)
    return jax.shard_map(
        on_device, mesh=mesh, in_specs=in_specs, out_specs=out_specs, check_vma=False
    )
```

time: 211 us -> 102 us (0.48)
  Pallas kernels: 0 us -> 94 us
  waiting for transfers between devices: 85.7 us -> 0 us
  matrix products: 45.8 us -> 0.86 us
  blocking collectives: 30.1 us -> 0 us
  between operations: 29.5 us -> 0.85 us
  starting transfers between devices: 7.01 us -> 0 us
  other arithmetic: 6.18 us -> 1.85 us
    pallas_call x0 -> x2, Pallas kernels: none -> 94 us  [the longest x1 50.2 us: expert_call(): pl.pallas_call(functools.partial(expert_kernel, ctx_count, exp_count), ou...]
    reduce_scatter x1 -> x0, waiting for transfers between devices: 61.9 us -> none  [on_device(): lax.psum_scatter(head_term.astype(jnp.bfloat16), 'exp', scatter_dimension...]
    dot_general x20 -> x1, matrix products: 45.4 us -> 0.35 us  [on_device(): jnp.dot(to_token, normed, preferred_element_type=jnp.float32)]
    all_to_all x1 -> x0, waiting for transfers between devices: 23.8 us -> none  [on_device(): lax.all_to_all(partials, ('ctx', 'exp'), split_axis=0, concat_axis=0, til...]
    all_to_all x1 -> x0, blocking collectives: 16.7 us -> none  [on_device(): lax.all_to_all(buffer.reshape(expert_count, capacity, model_width), 'exp'...]
    all_gather x1 -> x0, blocking collectives: 13.4 us -> none  [on_device(): lax.all_gather(sectioned.reshape(expert_count * capacity, model_width), '...]
    all_to_all x1 -> x0, starting transfers between devices: 3.97 us -> none  [on_device(): lax.all_to_all(partials, ('ctx', 'exp'), split_axis=0, concat_axis=0, til...]
    ppermute x2 -> x0, starting transfers between devices: 3.04 us -> none  [shifted(): lax.ppermute(value, axis, [(i, (i + by) % devices) for i in range(devices)])]
  transfers between devices with their start and end apart: 4 -> 0, of which waited for: 2 -> 0; matrix products, arithmetic and copies ran while one was open for 5% -> 0% of each run, Pallas kernels for 0% -> 0%
where the time goes in v1:
time: 102 us
  Pallas kernels  94 us (92%)
  local copies, waits for them, and re-layouts  4.39 us (4%)
  other arithmetic  1.85 us (2%)
    pallas_call x1, Pallas kernels, expert_call(): pl.pallas_call(functools.partial(expert_kernel, ctx_count, exp_count), ou...  50.2 us
    pallas_call x1, Pallas kernels, attention_call(): pl.pallas_call(functools.partial(attention_kernel, ctx_count, exp_count),...  43.8 us

profile of v1, /device:TPU:0, one launch (start us, length us, event | category | flops | bytes accessed | tf_op | source)
XLA Modules:
  0.0 102.0 jit_solution(1822898194516014049)
XLA Ops:
  0.0 0.8 constant_dynamic-slice_fusion
  0.8 0.1 concatenate.19
  0.9 0.1 slice_bitcast_fusion
  0.9 0.1 copy.29
  1.1 0.0 copy-start.4
  1.1 0.1 not_and_fusion
  1.2 0.1 and.59
  1.2 0.1 or.20
  1.3 0.1 or.23
  1.4 0.2 or.24
  1.6 0.1 and_convert_fusion.mask_ref
  1.7 0.3 copy.28
  2.7 0.1 compare_select_fusion.1
  2.7 0.1 broadcast_bitcast_fusion
  2.8 0.1 fusion.4.lat_ref
  3.0 43.8 %shard_map.145 = f32[8,7168]{1,0:T(8,128)S(1)} custom-call(bf16[512,576]{1,0:T(8,128)(2,1)S(1)} %bitcast.16, bf16[576,512]{1,0:T(8,128)(2,1)S(1)} %fusion.4.lat_ref, f32[128,1024]{1,0:T(8,128)S(1)} %and_convert_fusion.mask_ref, bf16[4,512,128]{2,1,0:T(8,128)(2,1)S(1)} %copy-done.1, bf16[512,7168]{1,0:T(8,128)(2,1)} %w_hbm.1), custom_call_target="tpu_custom_call" | custom-call | tf_op jit(solution)/shard_map/pallas_call | solution.py:213
  46.8 0.2 fusion.5
  47.0 0.3 fusion.3
  47.3 0.2 select_reduce_fusion
  47.5 0.1 copy.30
  47.6 0.1 reshape.201
  47.7 0.1 fusion.11
  47.8 0.2 select_reduce_fusion.2
  48.0 0.1 reduce_sum.63
  48.1 0.1 copy.32
  48.1 0.1 fusion.15
  48.2 0.3 convolution_convert_fusion
  48.6 1.0 reshape.202.buf_ref
  49.6 50.2 %shard_map.146 = bf16[16,16,896]{2,1,0:T(8,128)(2,1)} custom-call(bf16[16,16,896]{2,1,0:T(8,128)(2,1)} %reshape.202.buf_ref, bf16[1,7168,1024]{2,1,0:T(8,128)(2,1)} %gate_hbm.1, bf16[1,7168,1024]{2,1,0:T(8,128)(2,1)} %up_hbm.1, bf16[1,1024,7168]{2,1,0:T(8,128)(2,1)} %down_hbm.1), custom_call_target="tpu_custom_call" | custom-call | tf_op jit(solution)/shard_map/pallas_call | solution.py:415
  99.8 1.2 %reshape.204 = bf16[32,7168,1]{1,0,2:T(8,128)(2,1)S(1)} reshape(bf16[16,16,896]{2,1,0:T(8,128)(2,1)} %shard_map.146) | data formatting | bytes 917504 | tf_op jit(solution)/shard_map/reshape | solution.py:523
  101.0 0.3 fusion
  101.3 0.7 fusion.8
  (26 shorter events, 0.2 us)
Async XLA Ops:
  0.0 47.0 %copy-start = (bf16[7168,16]{0,1:T(8,128)(2,1)S(1)}, bf16[7168,16]{0,1:T(8,128)(2,1)}, u32[]{:S(2)}) copy-start(bf16[7168,16]{0,1:T(8,128)(2,1)} %param.25) | copy-start | bytes 688132
  0.0 1.7 %copy-start.2 = (bf16[128,4,576]{0,2,1:T(8,128)(2,1)S(1)}, bf16[128,4,576]{0,2,1:T(8,128)(2,1)}, u32[]{:S(2)}) copy-start(bf16[128,4,576]{0,2,1:T(8,128)(2,1)} %param.15) | copy-start | bytes 1769476
  1.0 1.6 %copy-start.8 = (s32[3]{0:T(128)S(1)}, s32[3]{0:T(128)}, u32[]{:S(2)}) copy-start(s32[3]{0:T(128)} %param.18) | copy-start | bytes 40
  1.0 1.8 %copy-start.3 = (bf16[384,576]{0,1:T(8,128)(2,1)S(1)}, bf16[384,576]{0,1:T(8,128)(2,1)}, u32[]{:S(2)}) copy-start(bf16[384,576]{0,1:T(8,128)(2,1)} %param.16) | copy-start | bytes 1327108
  1.1 1.8 %copy-start.4 = (bf16[128,576]{0,1:T(8,128)(2,1)S(1)}, bf16[128,576]{0,1:T(8,128)(2,1)}, u32[]{:S(2)}) copy-start(bf16[128,576]{0,1:T(8,128)(2,1)} %param.17) | copy-start | bytes 442372
  1.7 1.2 %copy-start.1 = (bf16[4,512,128]{2,1,0:T(8,128)(2,1)S(1)}, bf16[4,512,128]{2,1,0:T(8,128)(2,1)}, u32[]{:S(2)}) copy-start(bf16[4,512,128]{2,1,0:T(8,128)(2,1)} %up_ref.1) | copy-start | bytes 1572868
  2.9 43.9 %copy-start.5 = (bf16[8,7168]{1,0:T(8,128)(2,1)S(1)}, bf16[8,7168]{1,0:T(8,128)(2,1)}, u32[]{:S(2)}) copy-start(bf16[8,7168]{1,0:T(8,128)(2,1)} %param.23) | copy-start | bytes 344068
  3.0 44.0 %copy-start.6 = (bf16[7168]{0:T(1024)(128)(2,1)S(1)}, bf16[7168]{0:T(1024)(128)(2,1)}, u32[]{:S(2)}) copy-start(bf16[7168]{0:T(1024)(128)(2,1)} %param.24) | copy-start | bytes 43012
  3.0 44.3 %copy-start.7 = (s32[8,2]{0,1:T(2,128)S(1)}, s32[8,2]{0,1:T(2,128)}, u32[]{:S(2)}) copy-start(s32[8,2]{0,1:T(2,128)} %param.26) | copy-start | bytes 196

commit v2 on v1

--- a/solution.py
+++ b/solution.py
@@ -55,6 +55,23 @@
     bits = [lax.rem(exp // (1 << i), 2) for i in range(stages)]
     partners = [exp + (1 - 2 * bits[i]) * (1 << i) for i in range(stages)]
 
+    others = [lax.rem(ctx + d, ctx_count) for d in range(1, ctx_count)]
+    senders = [lax.rem(ctx + ctx_count - d, ctx_count) for d in range(1, ctx_count)]
+    greet([(o, exp) for o in others] + [(ctx, p) for p in partners])
+
+    part = pl.ds(pl.multiple_of(bits[0] * half, half), half)
+    sends = []
+    for d, other in enumerate(others):
+        copy = pltpu.make_async_remote_copy(
+            src_ref=lat_ref.at[part],
+            dst_ref=keys.at[ctx, part],
+            send_sem=lat_send.at[d],
+            recv_sem=lat_recv.at[d],
+            device_id=(other, exp),
+            device_id_type=MESH,
+        )
+        copy.start()
+        sends.append(copy)
     weights_in = []
     for chunk in range(CHUNKS):
         pair = []
@@ -67,24 +84,26 @@
             pair.append(copy)
         weights_in.append(pair)
 
-    others = [lax.rem(ctx + d, ctx_count) for d in range(1, ctx_count)]
-    senders = [lax.rem(ctx + ctx_count - d, ctx_count) for d in range(1, ctx_count)]
-    greet([(o, exp) for o in others] + [(ctx, p) for p in partners])
-
-    part = pl.ds(pl.multiple_of(bits[0] * half, half), half)
-    sends = []
-    for d, other in enumerate(others):
-        copy = pltpu.make_async_remote_copy(
-            src_ref=lat_ref.at[part],
-            dst_ref=keys.at[ctx, part],
-            send_sem=lat_send.at[d],
-            recv_sem=lat_recv.at[d],
-            device_id=(other, exp),
-            device_id_type=MESH,
-        )
-        copy.start()
-        sends.append(copy)
-    keys[ctx] = lat_ref[...]
+
+    factor = 1.0 / (NOPE + ROPE) ** 0.5
+
+    def attend(h, key_block, live):
+        q_head = q_ref[h * rows : (h + 1) * rows, :]
+        raw = jnp.dot(q_head, key_block[...], preferred_element_type=jnp.float32) * factor
+        raw = jnp.where(live, raw, -1e30)
+        top = jnp.max(raw, axis=1, keepdims=True)
+        weights = jnp.where(live, jnp.exp(raw - top), 0.0)
+        total = jnp.sum(weights, axis=1, keepdims=True)
+        mixture = lax.dot_general(
+            weights.astype(jnp.bfloat16),
+            key_block[:latent_width, :],
+            (((1,), (1,)), ((), ())),
+            preferred_element_type=jnp.float32,
+        )
+        return top, total, mixture
+
+    live = mask_ref[ctx] > 0
+    states = [attend(h, lat_ref, live) for h in range(heads)]
     forwards = []
     for d, sender in enumerate(senders):
         sends[d].wait_recv()
@@ -98,32 +117,22 @@
         )
         copy.start()
         forwards.append(copy)
-    for copy in forwards:
-        copy.wait_recv()
-
-    factor = 1.0 / (NOPE + ROPE) ** 0.5
+    for d, sender in enumerate(senders):
+        forwards[d].wait_recv()
+        live = mask_ref[sender] > 0
+        for h in range(heads):
+            top, total, mixture = states[h]
+            new_top, new_total, new_mixture = attend(h, keys.at[sender], live)
+            both_top = jnp.maximum(top, new_top)
+            shrink = jnp.exp(top - both_top)
+            new_shrink = jnp.exp(new_top - both_top)
+            states[h] = (
+                both_top,
+                total * shrink + new_total * new_shrink,
+                mixture * shrink + new_mixture * new_shrink,
+            )
     for h in range(heads):
-        q_head = q_ref[h * rows : (h + 1) * rows, :]
-        scores = []
-        for o in range(ctx_count):
-            raw = jnp.dot(q_head, keys[o], preferred_element_type=jnp.float32) * factor
-            live = mask_ref[:, o * key_rows : (o + 1) * key_rows] > 0
-            scores.append(jnp.where(live, raw, -1e30))
-        top = jnp.max(scores[0], axis=1, keepdims=True)
-        for s in scores[1:]:
-            top = jnp.maximum(top, jnp.max(s, axis=1, keepdims=True))
-        total = jnp.zeros((rows, 1), jnp.float32)
-        mixture = jnp.zeros((rows, latent_width), jnp.float32)
-        for o in range(ctx_count):
-            live = mask_ref[:, o * key_rows : (o + 1) * key_rows] > 0
-            weights = jnp.where(live, jnp.exp(scores[o] - top), 0.0)
-            total = total + jnp.sum(weights, axis=1, keepdims=True)
-            mixture = mixture + lax.dot_general(
-                weights.astype(jnp.bfloat16),
-                keys[o, :latent_width, :],
-                (((1,), (1,)), ((), ())),
-                preferred_element_type=jnp.float32,
-            )
+        top, total, mixture = states[h]
         attended = (mixture / total).astype(jnp.bfloat16)
         head_out = jnp.dot(attended, up_ref[h], preferred_element_type=jnp.float32)
         flat[:, h * vhead : (h + 1) * vhead] = head_out.astype(jnp.bfloat16)
@@ -153,7 +162,7 @@
             both = jnp.concatenate(sides, axis=1).astype(jnp.bfloat16)
             held[0][turn] = both.reshape(exp_count // 2, 2, 2 * tokens, width)
             exchange(0, turn).start()
-        for stage in reversed(range(stages)):
+        for stage in range(stages):
             chunk = turn - 1 - stage
             if chunk < 0 or chunk >= CHUNKS:
                 continue
@@ -268,12 +277,30 @@
                 down_hbm.at[0, :, span], down_w.at[:, span], w_sem.at[2, piece]
             )
         )
-    for copy in weights_in:
-        copy.start()
-
-    order = sorted(range(1, exp_count), key=lambda k: abs(k - exp_count // 2))
-    to = {k: lax.rem(exp + k, exp_count) for k in range(exp_count)}
-    origin = {k: lax.rem(exp + exp_count - k, exp_count) for k in range(exp_count)}
+    pending = [w for piece in range(PIECES) for w in (weights_in[piece], weights_in[PIECES + piece])]
+    pending = pending + weights_in[2 * PIECES :]
+
+    def fetch(count):
+        for copy in pending[:count]:
+            copy.start()
+        del pending[:count]
+
+    fetch(PIECES)
+    stages = exp_count.bit_length() - 1
+    to = {}
+    for k in range(exp_count):
+        partner = exp
+        for i in range(stages):
+            if (k >> i) & 1:
+                partner = partner + (1 - 2 * lax.rem(exp // (1 << i), 2)) * (1 << i)
+        to[k] = partner
+    origin = to
+    quarter = exp_count // 4
+    near_last = [2, 3, 1, 0]
+    rounds = [[8, 12, 4, 0][n] * exp_count // 16 + m for m in range(quarter) for n in range(4)]
+    order = [k for k in rounds if k >= quarter]
+    back_order = order + [k for k in near_last + list(range(4, quarter)) if k > 0]
+    order = [1] + [k for k in rounds if k > 1]
     others = [lax.rem(ctx + d, ctx_count) for d in range(1, ctx_count)]
     senders = [lax.rem(ctx + ctx_count - d, ctx_count) for d in range(1, ctx_count)]
     greet([(ctx, to[k]) for k in order] + [(o, exp) for o in others])
@@ -323,11 +350,13 @@
     recv[ctx, exp] = buf_ref[exp]
     for d in range(ctx_count - 1):
         forward(d, 0).start()
-    arrival = sorted(range(1, exp_count), key=lambda k: min(k, exp_count - k))
-    for k in arrival:
+    fetch(PIECES // 2)
+    for k in order:
         dispatch(k).wait_recv()
         for d in range(ctx_count - 1):
             forward(d, k).start()
+        fetch(1)
+    fetch(len(pending))
 
     row = lax.broadcasted_iota(jnp.int32, (exp_count * block, exp_count * block), 0)
     column = lax.broadcasted_iota(jnp.int32, (exp_count * block, exp_count * block), 1)
@@ -347,7 +376,7 @@
 
     spread(ctx)
     for d in range(ctx_count - 1):
-        for k in [0] + arrival:
+        for k in [0] + order:
             forward(d, k).wait_recv()
         spread(senders[d])
 
@@ -383,10 +412,10 @@
 
     for d in range(ctx_count - 1):
         gather(others[d])
-        for k in order + [0]:
+        for k in back_order + [0]:
             give_back(d, k).start()
     gather(ctx)
-    for k in order + [0]:
+    for k in back_order + [0]:
         total = recv[ctx, to[k]].astype(jnp.float32)
         for d in range(ctx_count - 1):
             give_back(d, k).wait_recv()
@@ -483,10 +512,10 @@
     later = jnp.logical_and(is_fresh, jnp.arange(ctx_count)[:, None] > ctx_index)
     live = jnp.logical_and(live, jnp.logical_not(later))
     allowed = jnp.logical_and(
-        live[None, :, :, None],
-        jnp.logical_or(jnp.logical_not(diagonal)[None, :, :, None], causal[:, None, None, :]),
+        live[:, None, :, None],
+        jnp.logical_or(jnp.logical_not(diagonal)[:, None, :, None], causal[None, :, None, :]),
     )
-    mask = allowed.reshape(rows_block, ctx_count * own_blocks * rows_block).astype(jnp.float32)
+    mask = allowed.reshape(ctx_count, rows_block, own_blocks * rows_block).astype(jnp.float32)
 
     attention = attention_call(
         ctx_count, exp_count, q_rows, latent_t, mask, value_up, output_weight

time: 102 us -> 92.3 us (0.905)
  Pallas kernels: 94 us -> 84 us
    pallas_call x1, Pallas kernels: 43.8 us -> 37.7 us  [attention_call(): pl.pallas_call(functools.partial(attention_kernel, ctx_count, exp_count),...]
    pallas_call x1, Pallas kernels: 50.2 us -> 46.3 us  [expert_call(): pl.pallas_call(functools.partial(expert_kernel, ctx_count, exp_count), ou...]
where the time goes in v2:
time: 92.3 us; the launch traced here: 91.8 us
  Pallas kernels  84 us (91%)
  local copies, waits for them, and re-layouts  4.29 us (5%)
  other arithmetic  1.84 us (2%)
    pallas_call x1, Pallas kernels, expert_call(): pl.pallas_call(functools.partial(expert_kernel, ctx_count, exp_count), ou...  46.3 us
    pallas_call x1, Pallas kernels, attention_call(): pl.pallas_call(functools.partial(attention_kernel, ctx_count, exp_count),...  37.7 us

profile of v2, /device:TPU:0, one launch (start us, length us, event | category | flops | bytes accessed | tf_op | source)
XLA Modules:
  0.0 91.8 jit_solution(8030640972379611248)
XLA Ops:
  0.0 0.8 constant_dynamic-slice_fusion
  0.8 0.1 concatenate.19
  0.9 0.1 slice_bitcast_fusion
  1.0 0.1 copy.29
  1.1 0.1 not_and_fusion
  1.2 0.1 broadcast_bitcast_fusion
  1.3 0.1 broadcast_bitcast_fusion.1
  1.4 0.1 or.25
  1.5 0.1 and_convert_fusion.mask_ref
  1.6 0.0 copy-start.1
  1.6 0.3 copy.28
  2.6 0.1 compare_select_fusion.1
  2.6 0.1 broadcast_bitcast_fusion.2
  2.7 0.1 fusion.4.lat_ref
  2.8 0.0 copy-start.5
  2.9 37.7 %shard_map.145 = f32[8,7168]{1,0:T(8,128)S(1)} custom-call(bf16[512,576]{1,0:T(8,128)(2,1)S(1)} %bitcast.28, bf16[576,512]{1,0:T(8,128)(2,1)S(1)} %fusion.4.lat_ref, f32[2,128,512]{2,1,0:T(8,128)S(1)} %and_convert_fusion.mask_ref, bf16[4,512,128]{2,1,0:T(8,128)(2,1)S(1)} %copy-done.1, bf16[512,7168]{1,0:T(8,128)(2,1)} %w_hbm.1), custom_call_target="tpu_custom_call" | custom-call | tf_op jit(solution)/shard_map/pallas_call | solution.py:222
  40.6 0.2 fusion.5
  40.8 0.3 fusion.3
  41.0 0.2 select_reduce_fusion
  41.2 0.1 copy.30
  41.3 0.1 reshape.192
  41.4 0.1 fusion.11
  41.5 0.2 select_reduce_fusion.2
  41.7 0.1 reduce_sum.63
  41.8 0.1 copy.32
  41.9 0.1 fusion.15
  42.0 0.3 convolution_convert_fusion
  42.3 1.0 %reshape.193.buf_ref = bf16[16,16,896]{2,1,0:T(8,128)(2,1)} reshape(bf16[32,7168]{1,0:T(8,128)(2,1)S(1)} %convolution_convert_fusion) | data formatting | bytes 917504 | tf_op jit(solution)/shard_map/reshape | solution.py:548
  43.3 46.3 %shard_map.146 = bf16[16,16,896]{2,1,0:T(8,128)(2,1)} custom-call(bf16[16,16,896]{2,1,0:T(8,128)(2,1)} %reshape.193.buf_ref, bf16[1,7168,1024]{2,1,0:T(8,128)(2,1)} %gate_hbm.1, bf16[1,7168,1024]{2,1,0:T(8,128)(2,1)} %up_hbm.1, bf16[1,1024,7168]{2,1,0:T(8,128)(2,1)} %down_hbm.1), custom_call_target="tpu_custom_call" | custom-call | tf_op jit(solution)/shard_map/pallas_call | solution.py:444
  89.6 1.2 %reshape.195 = bf16[32,7168,1]{1,0,2:T(8,128)(2,1)S(1)} reshape(bf16[16,16,896]{2,1,0:T(8,128)(2,1)} %shard_map.146) | data formatting | bytes 917504 | tf_op jit(solution)/shard_map/reshape | solution.py:552
  90.9 0.3 fusion
  91.1 0.7 fusion.8
  (28 shorter events, 0.2 us)
Async XLA Ops:
  0.0 40.8 %copy-start = (bf16[7168,16]{0,1:T(8,128)(2,1)S(1)}, bf16[7168,16]{0,1:T(8,128)(2,1)}, u32[]{:S(2)}) copy-start(bf16[7168,16]{0,1:T(8,128)(2,1)} %param.25) | copy-start | bytes 688132
  0.0 1.6 %copy-start.2 = (bf16[128,4,576]{0,2,1:T(8,128)(2,1)S(1)}, bf16[128,4,576]{0,2,1:T(8,128)(2,1)}, u32[]{:S(2)}) copy-start(bf16[128,4,576]{0,2,1:T(8,128)(2,1)} %param.15) | copy-start | bytes 1769476
  0.0 2.6 %copy-start.8 = (s32[3]{0:T(128)S(1)}, s32[3]{0:T(128)}, u32[]{:S(2)}) copy-start(s32[3]{0:T(128)} %param.18) | copy-start | bytes 40
  0.0 2.7 %copy-start.3 = (bf16[384,576]{0,1:T(8,128)(2,1)S(1)}, bf16[384,576]{0,1:T(8,128)(2,1)}, u32[]{:S(2)}) copy-start(bf16[384,576]{0,1:T(8,128)(2,1)} %param.16) | copy-start | bytes 1327108
  0.0 2.7 %copy-start.4 = (bf16[128,576]{0,1:T(8,128)(2,1)S(1)}, bf16[128,576]{0,1:T(8,128)(2,1)}, u32[]{:S(2)}) copy-start(bf16[128,576]{0,1:T(8,128)(2,1)} %param.17) | copy-start | bytes 442372
  1.6 1.2 %copy-start.1 = (bf16[4,512,128]{2,1,0:T(8,128)(2,1)S(1)}, bf16[4,512,128]{2,1,0:T(8,128)(2,1)}, u32[]{:S(2)}) copy-start(bf16[4,512,128]{2,1,0:T(8,128)(2,1)} %up_ref.1) | copy-start | bytes 1572868
  2.8 37.7 %copy-start.5 = (bf16[8,7168]{1,0:T(8,128)(2,1)S(1)}, bf16[8,7168]{1,0:T(8,128)(2,1)}, u32[]{:S(2)}) copy-start(bf16[8,7168]{1,0:T(8,128)(2,1)} %param.23) | copy-start | bytes 344068
  2.9 37.9 %copy-start.6 = (bf16[7168]{0:T(1024)(128)(2,1)S(1)}, bf16[7168]{0:T(1024)(128)(2,1)}, u32[]{:S(2)}) copy-start(bf16[7168]{0:T(1024)(128)(2,1)} %param.24) | copy-start | bytes 43012
  2.9 38.1 %copy-start.7 = (s32[8,2]{0,1:T(2,128)S(1)}, s32[8,2]{0,1:T(2,128)}, u32[]{:S(2)}) copy-start(s32[8,2]{0,1:T(2,128)} %param.26) | copy-start | bytes 196

commit v3 on v2

--- a/solution.py
+++ b/solution.py
@@ -10,7 +10,8 @@
 ROPE = 64
 NOPE = 128
 MESH = pl.DeviceIdType.MESH
-CHUNKS = 4
+CHUNKS = 7
+SWAPPED = (1, 4)
 PIECES = 8
 
 
@@ -139,13 +140,19 @@
 
     tokens = rows // exp_count
 
+    def axis_of(stage, chunk):
+        if chunk in SWAPPED and stage in (1, 2) and stages > 2:
+            return 3 - stage
+        return stage
+
     def exchange(stage, chunk):
+        bit = axis_of(stage, chunk)
         return pltpu.make_async_remote_copy(
-            src_ref=held[stage].at[chunk, :, 1 - bits[stage]],
+            src_ref=held[stage].at[chunk, :, 1 - bits[bit]],
             dst_ref=landed[stage].at[chunk],
             send_sem=rs_send.at[stage, chunk],
             recv_sem=rs_recv.at[stage, chunk],
-            device_id=(ctx, partners[stage]),
+            device_id=(ctx, partners[bit]),
             device_id_type=MESH,
         )
 
@@ -167,10 +174,19 @@
             if chunk < 0 or chunk >= CHUNKS:
                 continue
             exchange(stage, chunk).wait_recv()
-            mine = held[stage][chunk, :, pl.ds(bits[stage], 1)]
+            mine = held[stage][chunk, :, pl.ds(bits[axis_of(stage, chunk)], 1)]
             count = mine.shape[0]
             summed = mine.reshape(count, 2 * tokens, width).astype(jnp.float32)
             summed = summed + landed[stage][chunk].astype(jnp.float32)
+            if stage == 0 and axis_of(1, chunk) != 1:
+                summed = jnp.stack(
+                    [
+                        summed[b * 4 + second * 2 + first]
+                        for b in range(count // 4)
+                        for first in range(2)
+                        for second in range(2)
+                    ]
+                )
             if stage + 1 < stages:
                 held[stage + 1][chunk] = summed.astype(jnp.bfloat16).reshape(
                     count // 2, 2, 2 * tokens, width
@@ -234,11 +250,14 @@
 def expert_kernel(
     ctx_count,
     exp_count,
-    buf_ref,
+    pick_ref,
+    stack_ref,
     gate_hbm,
     up_hbm,
     down_hbm,
     out_ref,
+    buf_ref,
+    back,
     gate_w,
     up_w,
     down_w,
@@ -286,6 +305,14 @@
         del pending[:count]
 
     fetch(PIECES)
+    routes = pick_ref.shape[0] // stack_ref.shape[0]
+    placed = lax.dot_general(
+        pick_ref[...],
+        jnp.concatenate([stack_ref[...]] * routes, axis=0),
+        (((0,), (0,)), ((), ())),
+        preferred_element_type=jnp.float32,
+    )
+    buf_ref[...] = placed.astype(jnp.bfloat16).reshape(exp_count, block, width)
     stages = exp_count.bit_length() - 1
     to = {}
     for k in range(exp_count):
@@ -338,7 +365,7 @@
     def hand_in(k):
         return pltpu.make_async_remote_copy(
             src_ref=out_buf.at[to[k]],
-            dst_ref=out_ref.at[exp],
+            dst_ref=back.at[exp],
             send_sem=b_send.at[k],
             recv_sem=b_recv.at[k],
             device_id=(ctx, to[k]),
@@ -351,21 +378,21 @@
     for d in range(ctx_count - 1):
         forward(d, 0).start()
     fetch(PIECES // 2)
+    row = lax.broadcasted_iota(jnp.int32, (exp_count * block, exp_count * block), 0)
+    column = lax.broadcasted_iota(jnp.int32, (exp_count * block, exp_count * block), 1)
+    span_bits = slots.bit_length() - 1
+    split = jnp.where(
+        column == (row & (slots - 1)) * PIECES + (row >> span_bits), 1.0, 0.0
+    ).astype(jnp.bfloat16)
+    merge = jnp.where(
+        row == (column & (slots - 1)) * PIECES + (column >> span_bits), 1.0, 0.0
+    ).astype(jnp.bfloat16)
     for k in order:
         dispatch(k).wait_recv()
         for d in range(ctx_count - 1):
             forward(d, k).start()
         fetch(1)
     fetch(len(pending))
-
-    row = lax.broadcasted_iota(jnp.int32, (exp_count * block, exp_count * block), 0)
-    column = lax.broadcasted_iota(jnp.int32, (exp_count * block, exp_count * block), 1)
-    split = jnp.where(
-        column == lax.rem(row, slots) * PIECES + row // slots, 1.0, 0.0
-    ).astype(jnp.bfloat16)
-    merge = jnp.where(
-        row == lax.rem(column, slots) * PIECES + column // slots, 1.0, 0.0
-    ).astype(jnp.bfloat16)
 
     def spread(which):
         packed = recv[which].reshape(exp_count * block, width)
@@ -421,12 +448,15 @@
             give_back(d, k).wait_recv()
             total = total + ret_in[d, to[k]].astype(jnp.float32)
         if k == 0:
-            out_ref[exp] = total.astype(jnp.bfloat16)
+            back[exp] = total.astype(jnp.bfloat16)
         else:
             out_buf[to[k]] = total.astype(jnp.bfloat16)
             hand_in(k).start()
     for k in order:
         hand_in(k).wait_recv()
+    packed = back[...].reshape(exp_count * block, width)
+    taken = jnp.dot(pick_ref[...], packed, preferred_element_type=jnp.float32)
+    out_ref[...] = taken.astype(jnp.bfloat16)
     for k in order:
         hand_in(k).wait_send()
     for d in range(ctx_count - 1):
@@ -434,8 +464,9 @@
             give_back(d, k).wait_send()
 
 
-def expert_call(ctx_count, exp_count, buffer, gate_weight, up_weight, down_weight):
-    block, width = buffer.shape[1:]
+def expert_call(ctx_count, exp_count, pick, stack, gate_weight, up_weight, down_weight):
+    block = pick.shape[1] // exp_count
+    width = stack.shape[1]
     model, hidden = gate_weight.shape[1:]
     slots = exp_count * block // PIECES
     vmem = pl.BlockSpec(memory_space=pltpu.VMEM)
@@ -443,10 +474,12 @@
     dma = pltpu.SemaphoreType.DMA
     return pl.pallas_call(
         functools.partial(expert_kernel, ctx_count, exp_count),
-        out_shape=jax.ShapeDtypeStruct(buffer.shape, jnp.bfloat16),
-        in_specs=[vmem, anywhere, anywhere, anywhere],
+        out_shape=jax.ShapeDtypeStruct((pick.shape[0], width), jnp.bfloat16),
+        in_specs=[vmem, vmem, anywhere, anywhere, anywhere],
         out_specs=vmem,
         scratch_shapes=[
+            pltpu.VMEM((exp_count, block, width), jnp.bfloat16),
+            pltpu.VMEM((exp_count, block, width), jnp.bfloat16),
             pltpu.VMEM((model, hidden), jnp.bfloat16),
             pltpu.VMEM((model, hidden), jnp.bfloat16),
             pltpu.VMEM((hidden, model), jnp.bfloat16),
@@ -467,7 +500,7 @@
         compiler_params=pltpu.CompilerParams(
             collective_id=1, has_side_effects=True, vmem_limit_bytes=62 << 20
         ),
-    )(buffer, gate_weight, up_weight, down_weight)
+    )(pick, stack, gate_weight, up_weight, down_weight)
 
 
 def on_device(
@@ -538,22 +571,25 @@
     flat_hits = route_hits.reshape(token_count * route_count, expert_count).astype(jnp.int32)
     before = jnp.cumsum(flat_hits, axis=0) - flat_hits
     slot_index = jnp.sum(before * flat_hits, axis=1)
-    target = route_ids.reshape(-1) * capacity + slot_index
-    placing = (target[None, :] == jnp.arange(expert_count * capacity)[:, None]).astype(jnp.bfloat16)
-    to_token = jnp.sum(placing.reshape(-1, token_count, route_count), axis=2)
-    buffer = jnp.dot(to_token, normed, preferred_element_type=jnp.float32).astype(jnp.bfloat16)
-    summed = expert_call(
+    target = (route_ids.reshape(-1) * capacity + slot_index).reshape(token_count, route_count)
+    place = target.T[:, None, :] * PIECES + jnp.arange(PIECES)[None, :, None]
+    pick = (
+        place.reshape(-1)[:, None] == jnp.arange(expert_count * capacity * PIECES)[None, :]
+    ).astype(jnp.bfloat16)
+    width = model_width // PIECES
+    stack = normed.reshape(token_count, PIECES, width).transpose(1, 0, 2)
+    taken = expert_call(
         ctx_count,
         exp_count,
-        buffer.reshape(expert_count, capacity * PIECES, model_width // PIECES),
+        pick,
+        stack.reshape(PIECES * token_count, width),
         gate_weight,
         up_weight,
         down_weight,
-    ).reshape(expert_count * capacity, model_width)
-    gathered_back = jnp.dot(
-        jnp.transpose(placing), summed, preferred_element_type=jnp.float32
-    ).reshape(token_count, route_count, model_width)
-    expert_mix = jnp.sum(gate_values[:, :, None] * gathered_back, axis=1)
+    ).reshape(route_count, PIECES, token_count, width)
+    gates = gate_values.T[:, None, :, None]
+    expert_mix = jnp.sum(gates * taken.astype(jnp.float32), axis=0)
+    expert_mix = expert_mix.transpose(1, 0, 2).reshape(token_count, model_width)
     return (hidden_wide + expert_mix).astype(jnp.bfloat16)
 
 

time: 92.3 us -> 95.7 us (1.037)
  Pallas kernels: 84 us -> 88.7 us
  local copies, waits for them, and re-layouts: 4.29 us -> 2.19 us
  other arithmetic: 1.84 us -> 3.66 us
    pallas_call x1, Pallas kernels: 37.7 us -> 41.9 us  [attention_call(): pl.pallas_call(functools.partial(attention_kernel, ctx_count, exp_count),...]
    reshape x3 -> x0, local copies, waits for them, and re-layouts: 2.29 us -> none  [the longest x1 1.23 us: on_device(): summed = expert_call(ctx_count, exp_count, buffer.reshape(expert_count, c...]
    reduce_sum x1, other arithmetic: 0.08 us -> 1.07 us  [on_device(): expert_mix = jnp.sum(gates * taken.astype(jnp.float32), axis=0)]
where the time goes in v3:
time: 95.7 us; the launch traced here: 95.5 us
  Pallas kernels  88.7 us (93%)
  other arithmetic  3.66 us (4%)
  local copies, waits for them, and re-layouts  2.19 us (2%)
    pallas_call x1, Pallas kernels, expert_call(): pl.pallas_call(functools.partial(expert_kernel, ctx_count, exp_count), ou...  46.7 us
    pallas_call x1, Pallas kernels, attention_call(): pl.pallas_call(functools.partial(attention_kernel, ctx_count, exp_count),...  41.9 us

profile of v3, /device:TPU:0, one launch (start us, length us, event | category | flops | bytes accessed | tf_op | source)
XLA Modules:
  0.0 95.5 jit_solution(17120363596252285168)
XLA Ops:
  0.0 0.8 constant_dynamic-slice_fusion
  0.8 0.1 concatenate.19
  0.9 0.1 slice_bitcast_fusion
  1.0 0.1 copy.29
  1.1 0.1 not_and_fusion
  1.2 0.1 broadcast_bitcast_fusion
  1.3 0.1 broadcast_bitcast_fusion.1
  1.4 0.1 or.25
  1.5 0.1 and_convert_fusion.mask_ref
  1.6 0.0 copy-start.1
  1.6 0.3 copy.28
  2.6 0.1 compare_select_fusion.1
  2.6 0.1 broadcast_bitcast_fusion.2
  2.7 0.1 fusion.3.lat_ref
  2.8 0.0 copy-start.6
  2.9 0.0 copy-start.7
  2.9 41.9 %shard_map.145 = f32[8,7168]{1,0:T(8,128)S(1)} custom-call(bf16[512,576]{1,0:T(8,128)(2,1)S(1)} %bitcast.38, bf16[576,512]{1,0:T(8,128)(2,1)S(1)} %fusion.3.lat_ref, f32[2,128,512]{2,1,0:T(8,128)S(1)} %and_convert_fusion.mask_ref, bf16[4,512,128]{2,1,0:T(8,128)(2,1)S(1)} %copy-done.1, bf16[512,7168]{1,0:T(8,128)(2,1)} %w_hbm.1), custom_call_target="tpu_custom_call" | custom-call | tf_op jit(solution)/shard_map/pallas_call | solution.py:238
  44.8 0.2 fusion.5
  45.0 0.1 fusion.7
  45.1 0.2 fusion.2
  45.3 0.2 select_reduce_fusion
  45.5 0.1 copy.30
  45.6 0.1 eq.59
  45.7 0.1 fusion.10
  45.8 0.2 select_reduce_fusion.2
  46.0 0.1 reduce_sum.51
  46.1 0.1 copy.32
  46.2 0.1 add.53
  46.3 0.7 fusion.9.pick_ref
  47.0 46.7 %shard_map.146 = bf16[128,896]{1,0:T(8,128)(2,1)} custom-call(bf16[128,256]{1,0:T(8,128)(2,1)} %fusion.9.pick_ref, bf16[64,896]{1,0:T(8,128)(2,1)} %bitcast.39, bf16[1,7168,1024]{2,1,0:T(8,128)(2,1)} %gate_hbm.1, bf16[1,7168,1024]{2,1,0:T(8,128)(2,1)} %up_hbm.1, bf16[1,1024,7168]{2,1,0:T(8,128)(2,1)} %down_hbm.1), custom_call_target="tpu_custom_call" | custom-call | tf_op jit(solution)/shard_map/pallas_call | solution.py:475
  93.8 1.1 %fusion.4 = f32[8,8,896]{2,1,0:T(8,128)S(1)} fusion(bf16[2,8,8,896]{3,2,1,0:T(8,128)(2,1)} %bitcast.40, f32[2,8]{1,0:T(2,128)S(1)} %divide_bitcast_fusion), kind=kLoop, calls=%fused_computation.8 | loop fusion | flops 286720 | bytes 458816 | tf_op jit(solution)/shard_map/reduce_sum | solution.py:591
  94.8 0.7 fusion.8
  (30 shorter events, 0.2 us)
Async XLA Ops:
  0.0 45.1 %copy-start = (bf16[7168,16]{0,1:T(8,128)(2,1)S(1)}, bf16[7168,16]{0,1:T(8,128)(2,1)}, u32[]{:S(2)}) copy-start(bf16[7168,16]{0,1:T(8,128)(2,1)} %param.25) | copy-start | bytes 688132
  0.0 1.6 %copy-start.3 = (bf16[128,4,576]{0,2,1:T(8,128)(2,1)S(1)}, bf16[128,4,576]{0,2,1:T(8,128)(2,1)}, u32[]{:S(2)}) copy-start(bf16[128,4,576]{0,2,1:T(8,128)(2,1)} %param.15) | copy-start | bytes 1769476
  0.0 2.6 %copy-start.9 = (s32[3]{0:T(128)S(1)}, s32[3]{0:T(128)}, u32[]{:S(2)}) copy-start(s32[3]{0:T(128)} %param.18) | copy-start | bytes 40
  0.0 2.7 %copy-start.4 = (bf16[384,576]{0,1:T(8,128)(2,1)S(1)}, bf16[384,576]{0,1:T(8,128)(2,1)}, u32[]{:S(2)}) copy-start(bf16[384,576]{0,1:T(8,128)(2,1)} %param.16) | copy-start | bytes 1327108
  0.0 2.7 %copy-start.5 = (bf16[128,576]{0,1:T(8,128)(2,1)S(1)}, bf16[128,576]{0,1:T(8,128)(2,1)}, u32[]{:S(2)}) copy-start(bf16[128,576]{0,1:T(8,128)(2,1)} %param.17) | copy-start | bytes 442372
  1.6 1.2 %copy-start.1 = (bf16[4,512,128]{2,1,0:T(8,128)(2,1)S(1)}, bf16[4,512,128]{2,1,0:T(8,128)(2,1)}, u32[]{:S(2)}) copy-start(bf16[4,512,128]{2,1,0:T(8,128)(2,1)} %up_ref.1) | copy-start | bytes 1572868
  2.8 42.0 %copy-start.6 = (bf16[8,7168]{1,0:T(8,128)(2,1)S(1)}, bf16[8,7168]{1,0:T(8,128)(2,1)}, u32[]{:S(2)}) copy-start(bf16[8,7168]{1,0:T(8,128)(2,1)} %param.23) | copy-start | bytes 344068
  2.9 42.1 %copy-start.7 = (bf16[7168]{0:T(1024)(128)(2,1)S(1)}, bf16[7168]{0:T(1024)(128)(2,1)}, u32[]{:S(2)}) copy-start(bf16[7168]{0:T(1024)(128)(2,1)} %param.24) | copy-start | bytes 43012
  2.9 42.4 %copy-start.8 = (s32[8,2]{0,1:T(2,128)S(1)}, s32[8,2]{0,1:T(2,128)}, u32[]{:S(2)}) copy-start(s32[8,2]{0,1:T(2,128)} %param.26) | copy-start | bytes 196
  45.1 1.9 %copy-start.2 = (bf16[8,7168]{1,0:T(8,128)(2,1)}, bf16[8,7168]{1,0:T(8,128)(2,1)S(1)}, u32[]{:S(2)}) copy-start(bf16[8,7168]{1,0:T(8,128)(2,1)S(1)} %fusion.7) | copy-start | bytes 344068

commit v4 on v3

--- a/solution.py
+++ b/solution.py
@@ -10,8 +10,7 @@
 ROPE = 64
 NOPE = 128
 MESH = pl.DeviceIdType.MESH
-CHUNKS = 7
-SWAPPED = (1, 4)
+CHUNKS = 4
 PIECES = 8
 
 
@@ -140,19 +139,13 @@
 
     tokens = rows // exp_count
 
-    def axis_of(stage, chunk):
-        if chunk in SWAPPED and stage in (1, 2) and stages > 2:
-            return 3 - stage
-        return stage
-
     def exchange(stage, chunk):
-        bit = axis_of(stage, chunk)
         return pltpu.make_async_remote_copy(
-            src_ref=held[stage].at[chunk, :, 1 - bits[bit]],
+            src_ref=held[stage].at[chunk, :, 1 - bits[stage]],
             dst_ref=landed[stage].at[chunk],
             send_sem=rs_send.at[stage, chunk],
             recv_sem=rs_recv.at[stage, chunk],
-            device_id=(ctx, partners[bit]),
+            device_id=(ctx, partners[stage]),
             device_id_type=MESH,
         )
 
@@ -174,19 +167,10 @@
             if chunk < 0 or chunk >= CHUNKS:
                 continue
             exchange(stage, chunk).wait_recv()
-            mine = held[stage][chunk, :, pl.ds(bits[axis_of(stage, chunk)], 1)]
+            mine = held[stage][chunk, :, pl.ds(bits[stage], 1)]
             count = mine.shape[0]
             summed = mine.reshape(count, 2 * tokens, width).astype(jnp.float32)
             summed = summed + landed[stage][chunk].astype(jnp.float32)
-            if stage == 0 and axis_of(1, chunk) != 1:
-                summed = jnp.stack(
-                    [
-                        summed[b * 4 + second * 2 + first]
-                        for b in range(count // 4)
-                        for first in range(2)
-                        for second in range(2)
-                    ]
-                )
             if stage + 1 < stages:
                 held[stage + 1][chunk] = summed.astype(jnp.bfloat16).reshape(
                     count // 2, 2, 2 * tokens, width
@@ -321,13 +305,13 @@
             if (k >> i) & 1:
                 partner = partner + (1 - 2 * lax.rem(exp // (1 << i), 2)) * (1 << i)
         to[k] = partner
-    origin = to
     quarter = exp_count // 4
-    near_last = [2, 3, 1, 0]
-    rounds = [[8, 12, 4, 0][n] * exp_count // 16 + m for m in range(quarter) for n in range(4)]
-    order = [k for k in rounds if k >= quarter]
-    back_order = order + [k for k in near_last + list(range(4, quarter)) if k > 0]
-    order = [1] + [k for k in rounds if k > 1]
+    tops = [2 * quarter, 3 * quarter, quarter, 0]
+    pairs = [top + low for low in range(0, quarter, 2) for top in tops]
+    back_pairs = [p for p in pairs if p >= quarter] + [p for p in reversed(range(0, quarter, 2))]
+    pairs = [0] + [p for p in pairs if p > 0]
+    order = [k for p in pairs for k in (p, p + 1) if k > 0]
+    spans = {p: pl.ds(to[p] // 2 * 2, 2) for p in pairs}
     others = [lax.rem(ctx + d, ctx_count) for d in range(1, ctx_count)]
     senders = [lax.rem(ctx + ctx_count - d, ctx_count) for d in range(1, ctx_count)]
     greet([(ctx, to[k]) for k in order] + [(o, exp) for o in others])
@@ -342,22 +326,22 @@
             device_id_type=MESH,
         )
 
-    def forward(d, k):
+    def forward(d, p):
         return pltpu.make_async_remote_copy(
-            src_ref=recv.at[ctx, origin[k]],
-            dst_ref=recv.at[ctx, origin[k]],
-            send_sem=f_send.at[d, k],
-            recv_sem=f_recv.at[d, k],
+            src_ref=recv.at[ctx, spans[p]],
+            dst_ref=recv.at[ctx, spans[p]],
+            send_sem=f_send.at[d, p],
+            recv_sem=f_recv.at[d, p],
             device_id=(others[d], exp),
             device_id_type=MESH,
         )
 
-    def give_back(d, k):
+    def give_back(d, p):
         return pltpu.make_async_remote_copy(
-            src_ref=recv.at[others[d], to[k]],
-            dst_ref=ret_in.at[d, to[k]],
-            send_sem=r_send.at[d, k],
-            recv_sem=r_recv.at[d, k],
+            src_ref=recv.at[others[d], spans[p]],
+            dst_ref=ret_in.at[d, spans[p]],
+            send_sem=r_send.at[d, p],
+            recv_sem=r_recv.at[d, p],
             device_id=(others[d], exp),
             device_id_type=MESH,
         )
@@ -375,8 +359,6 @@
     for k in order:
         dispatch(k).start()
     recv[ctx, exp] = buf_ref[exp]
-    for d in range(ctx_count - 1):
-        forward(d, 0).start()
     fetch(PIECES // 2)
     row = lax.broadcasted_iota(jnp.int32, (exp_count * block, exp_count * block), 0)
     column = lax.broadcasted_iota(jnp.int32, (exp_count * block, exp_count * block), 1)
@@ -387,11 +369,13 @@
     merge = jnp.where(
         row == (column & (slots - 1)) * PIECES + (column >> span_bits), 1.0, 0.0
     ).astype(jnp.bfloat16)
-    for k in order:
-        dispatch(k).wait_recv()
+    for p in pairs:
+        for k in (p, p + 1):
+            if k > 0:
+                dispatch(k).wait_recv()
         for d in range(ctx_count - 1):
-            forward(d, k).start()
-        fetch(1)
+            forward(d, p).start()
+        fetch(2)
     fetch(len(pending))
 
     def spread(which):
@@ -403,8 +387,8 @@
 
     spread(ctx)
     for d in range(ctx_count - 1):
-        for k in [0] + order:
-            forward(d, k).wait_recv()
+        for p in pairs:
+            forward(d, p).wait_recv()
         spread(senders[d])
 
     gate = None
@@ -428,8 +412,8 @@
     for k in order:
         dispatch(k).wait_send()
     for d in range(ctx_count - 1):
-        for k in range(exp_count):
-            forward(d, k).wait_send()
+        for p in pairs:
+            forward(d, p).wait_send()
 
     def gather(which):
         at = pl.ds(pl.multiple_of(which * slots, slots), slots)
@@ -439,19 +423,21 @@
 
     for d in range(ctx_count - 1):
         gather(others[d])
-        for k in back_order + [0]:
-            give_back(d, k).start()
+        for p in back_pairs:
+            give_back(d, p).start()
     gather(ctx)
-    for k in back_order + [0]:
-        total = recv[ctx, to[k]].astype(jnp.float32)
+    for p in back_pairs:
         for d in range(ctx_count - 1):
-            give_back(d, k).wait_recv()
-            total = total + ret_in[d, to[k]].astype(jnp.float32)
-        if k == 0:
-            back[exp] = total.astype(jnp.bfloat16)
-        else:
-            out_buf[to[k]] = total.astype(jnp.bfloat16)
-            hand_in(k).start()
+            give_back(d, p).wait_recv()
+        for k in (p, p + 1):
+            total = recv[ctx, to[k]].astype(jnp.float32)
+            for d in range(ctx_count - 1):
+                total = total + ret_in[d, to[k]].astype(jnp.float32)
+            if k == 0:
+                back[exp] = total.astype(jnp.bfloat16)
+            else:
+                out_buf[to[k]] = total.astype(jnp.bfloat16)
+                hand_in(k).start()
     for k in order:
         hand_in(k).wait_recv()
     packed = back[...].reshape(exp_count * block, width)
@@ -460,8 +446,8 @@
     for k in order:
         hand_in(k).wait_send()
     for d in range(ctx_count - 1):
-        for k in range(exp_count):
-            give_back(d, k).wait_send()
+        for p in pairs:
+            give_back(d, p).wait_send()
 
 
 def expert_call(ctx_count, exp_count, pick, stack, gate_weight, up_weight, down_weight):

time: 95.7 us -> 94.8 us (level)
  Pallas kernels: 88.7 us -> 87.7 us
    pallas_call x1, Pallas kernels: 41.9 us -> 37.7 us  [attention_call(): pl.pallas_call(functools.partial(attention_kernel, ctx_count, exp_count),...]
    pallas_call x1, Pallas kernels: 46.7 us -> 50.1 us  [expert_call(): pl.pallas_call(functools.partial(expert_kernel, ctx_count, exp_count), ou...]
where the time goes in v4:
time: 94.8 us; the launch traced here: 94.6 us
  Pallas kernels  87.7 us (93%)
  other arithmetic  3.66 us (4%)
  local copies, waits for them, and re-layouts  2.19 us (2%)
    pallas_call x1, Pallas kernels, expert_call(): pl.pallas_call(functools.partial(expert_kernel, ctx_count, exp_count), ou...  50.1 us
    pallas_call x1, Pallas kernels, attention_call(): pl.pallas_call(functools.partial(attention_kernel, ctx_count, exp_count),...  37.7 us

profile of v4, /device:TPU:0, one launch (start us, length us, event | category | flops | bytes accessed | tf_op | source)
XLA Modules:
  0.0 94.6 jit_solution(6167990319216819225)
XLA Ops:
  0.0 0.8 constant_dynamic-slice_fusion
  0.8 0.1 concatenate.19
  0.9 0.1 slice_bitcast_fusion
  1.0 0.1 copy.29
  1.1 0.1 not_and_fusion
  1.2 0.1 broadcast_bitcast_fusion
  1.3 0.1 broadcast_bitcast_fusion.1
  1.4 0.1 or.25
  1.5 0.1 and_convert_fusion.mask_ref
  1.6 0.0 copy-start.1
  1.6 0.3 copy.28
  2.6 0.1 compare_select_fusion.1
  2.6 0.1 broadcast_bitcast_fusion.2
  2.7 0.1 fusion.3.lat_ref
  2.9 0.0 copy-start.7
  2.9 0.0 copy-start.8
  2.9 37.7 %shard_map.145 = f32[8,7168]{1,0:T(8,128)S(1)} custom-call(bf16[512,576]{1,0:T(8,128)(2,1)S(1)} %bitcast.38, bf16[576,512]{1,0:T(8,128)(2,1)S(1)} %fusion.3.lat_ref, f32[2,128,512]{2,1,0:T(8,128)S(1)} %and_convert_fusion.mask_ref, bf16[4,512,128]{2,1,0:T(8,128)(2,1)S(1)} %copy-done.1, bf16[512,7168]{1,0:T(8,128)(2,1)} %w_hbm.1), custom_call_target="tpu_custom_call" | custom-call | tf_op jit(solution)/shard_map/pallas_call | solution.py:222
  40.6 0.2 fusion.5
  40.8 0.1 fusion.7
  40.9 0.2 fusion.2
  41.1 0.2 select_reduce_fusion
  41.3 0.1 copy.30
  41.4 0.1 eq.59
  41.5 0.1 fusion.10
  41.6 0.2 select_reduce_fusion.2
  41.8 0.1 reduce_sum.51
  41.9 0.1 copy.32
  41.9 0.1 add.53
  42.1 0.7 fusion.9.pick_ref
  42.8 50.1 %shard_map.146 = bf16[128,896]{1,0:T(8,128)(2,1)} custom-call(bf16[128,256]{1,0:T(8,128)(2,1)} %fusion.9.pick_ref, bf16[64,896]{1,0:T(8,128)(2,1)} %bitcast.39, bf16[1,7168,1024]{2,1,0:T(8,128)(2,1)} %gate_hbm.1, bf16[1,7168,1024]{2,1,0:T(8,128)(2,1)} %up_hbm.1, bf16[1,1024,7168]{2,1,0:T(8,128)(2,1)} %down_hbm.1), custom_call_target="tpu_custom_call" | custom-call | tf_op jit(solution)/shard_map/pallas_call | solution.py:461
  92.9 1.1 %fusion.4 = f32[8,8,896]{2,1,0:T(8,128)S(1)} fusion(bf16[2,8,8,896]{3,2,1,0:T(8,128)(2,1)} %bitcast.40, f32[2,8]{1,0:T(2,128)S(1)} %divide_bitcast_fusion), kind=kLoop, calls=%fused_computation.8 | loop fusion | flops 286720 | bytes 458816 | tf_op jit(solution)/shard_map/reduce_sum | solution.py:577
  93.9 0.7 fusion.8
  (30 shorter events, 0.2 us)
Async XLA Ops:
  0.0 40.9 %copy-start = (bf16[7168,16]{0,1:T(8,128)(2,1)S(1)}, bf16[7168,16]{0,1:T(8,128)(2,1)}, u32[]{:S(2)}) copy-start(bf16[7168,16]{0,1:T(8,128)(2,1)} %param.25) | copy-start | bytes 688132
  0.0 1.6 %copy-start.3 = (bf16[128,4,576]{0,2,1:T(8,128)(2,1)S(1)}, bf16[128,4,576]{0,2,1:T(8,128)(2,1)}, u32[]{:S(2)}) copy-start(bf16[128,4,576]{0,2,1:T(8,128)(2,1)} %param.15) | copy-start | bytes 1769476
  0.0 2.6 %copy-start.9 = (s32[3]{0:T(128)S(1)}, s32[3]{0:T(128)}, u32[]{:S(2)}) copy-start(s32[3]{0:T(128)} %param.18) | copy-start | bytes 40
  0.0 2.7 %copy-start.4 = (bf16[384,576]{0,1:T(8,128)(2,1)S(1)}, bf16[384,576]{0,1:T(8,128)(2,1)}, u32[]{:S(2)}) copy-start(bf16[384,576]{0,1:T(8,128)(2,1)} %param.16) | copy-start | bytes 1327108
  0.0 2.7 %copy-start.5 = (bf16[128,576]{0,1:T(8,128)(2,1)S(1)}, bf16[128,576]{0,1:T(8,128)(2,1)}, u32[]{:S(2)}) copy-start(bf16[128,576]{0,1:T(8,128)(2,1)} %param.17) | copy-start | bytes 442372
  1.6 1.2 %copy-start.1 = (bf16[4,512,128]{2,1,0:T(8,128)(2,1)S(1)}, bf16[4,512,128]{2,1,0:T(8,128)(2,1)}, u32[]{:S(2)}) copy-start(bf16[4,512,128]{2,1,0:T(8,128)(2,1)} %up_ref.1) | copy-start | bytes 1572868
  2.8 37.7 %copy-start.6 = (bf16[8,7168]{1,0:T(8,128)(2,1)S(1)}, bf16[8,7168]{1,0:T(8,128)(2,1)}, u32[]{:S(2)}) copy-start(bf16[8,7168]{1,0:T(8,128)(2,1)} %param.23) | copy-start | bytes 344068
  2.9 37.9 %copy-start.7 = (bf16[7168]{0:T(1024)(128)(2,1)S(1)}, bf16[7168]{0:T(1024)(128)(2,1)}, u32[]{:S(2)}) copy-start(bf16[7168]{0:T(1024)(128)(2,1)} %param.24) | copy-start | bytes 43012
  2.9 38.2 %copy-start.8 = (s32[8,2]{0,1:T(2,128)S(1)}, s32[8,2]{0,1:T(2,128)}, u32[]{:S(2)}) copy-start(s32[8,2]{0,1:T(2,128)} %param.26) | copy-start | bytes 196
  40.9 1.9 %copy-start.2 = (bf16[8,7168]{1,0:T(8,128)(2,1)}, bf16[8,7168]{1,0:T(8,128)(2,1)S(1)}, u32[]{:S(2)}) copy-start(bf16[8,7168]{1,0:T(8,128)(2,1)S(1)} %fusion.7) | copy-start | bytes 344068
